TPU v7x, 128 devices: a whole 4x4x4 slice. The times are simulated.
128 devices in a mesh: dp: 16 (over y_lo, x, core), tensor: 8 (over y_hi, z).
Axes of the slice: x: 4, y: 4 (y_hi: 2, y_lo: 2; y = y_hi * 2 + y_lo), z: 4, core: 2. Of those that a mesh axis runs over, the one named last changes fastest.
Arguments:
- block_input: bfloat16 [16384, 2560], P(('dp', 'tensor')), may hold values from -6 to 6
- out_grad: bfloat16 [16384, 2560], P(('dp', 'tensor')), may hold values from -6 to 6
- norm_gains: float32 [6144], P(('dp', 'tensor')), may hold values from 0.5 to 1.5
- latent_weight: float32 [2560, 1056], P(('dp', 'tensor')), may hold values from -0.125 to 0.125
- query_weight: float32 [768, 3840], P('dp', 'tensor'), may hold values from -0.21875 to 0.21875
- keys_weight: float32 [256, 5120], P('dp', 'tensor'), may hold values from -0.375 to 0.375
- output_weight: float32 [2560, 2560], P('tensor', 'dp'), may hold values from -2 to 2
- gate_weight: float32 [2560, 6400], P('dp', 'tensor'), may hold values from -0.125 to 0.125
- up_weight: float32 [2560, 6400], P('dp', 'tensor'), may hold values from -0.125 to 0.125
- down_weight: float32 [6400, 2560], P('tensor', 'dp'), may hold values from -0.625 to 0.625
- gains_moment: float32 [6144], P(('dp', 'tensor')), may hold values from -48 to 48
- gains_second: float32 [6144], P(('dp', 'tensor')), may hold values from 294.912 to 1179.648
- latent_moment: float32 [2560, 1056], P(('dp', 'tensor')), may hold values from -32 to 32
- latent_second: float32 [2560, 1056], P(('dp', 'tensor')), may hold values from 131.072 to 524.288
- query_moment: float32 [768, 3840], P('dp', 'tensor'), may hold values from -16 to 16
- query_second: float32 [768, 3840], P('dp', 'tensor'), may hold values from 32.768 to 131.072
- keys_moment: float32 [256, 5120], P('dp', 'tensor'), may hold values from -40 to 40
- keys_second: float32 [256, 5120], P('dp', 'tensor'), may hold values from 204.8 to 819.2
- output_moment: float32 [2560, 2560], P('tensor', 'dp'), may hold values from -3.5 to 3.5
- output_second: float32 [2560, 2560], P('tensor', 'dp'), may hold values from 1.441792 to 5.7344
- gate_moment: float32 [2560, 6400], P('dp', 'tensor'), may hold values from -48 to 48
- gate_second: float32 [2560, 6400], P('dp', 'tensor'), may hold values from 245.76 to 983.04
- up_moment: float32 [2560, 6400], P('dp', 'tensor'), may hold values from -48 to 48
- up_second: float32 [2560, 6400], P('dp', 'tensor'), may hold values from 245.76 to 983.04
- down_moment: float32 [6400, 2560], P('tensor', 'dp'), may hold values from -8 to 8
- down_second: float32 [6400, 2560], P('tensor', 'dp'), may hold values from 9.33888 to 37.6832
Outputs:
- block_output: float32 [16384, 2560], P(('dp', 'tensor'))
- input_grad: float32 [16384, 2560], P(('dp', 'tensor'))
- next_gains: float32 [6144], P(('dp', 'tensor'))
- moment_gains: float32 [6144], P(('dp', 'tensor'))
- second_gains: float32 [6144], P(('dp', 'tensor'))
- next_latent: float32 [2560, 1056], P(('dp', 'tensor'))
- moment_latent: float32 [2560, 1056], P(('dp', 'tensor'))
- second_latent: float32 [2560, 1056], P(('dp', 'tensor'))
- next_query: float32 [768, 3840], P('dp', 'tensor')
- moment_query: float32 [768, 3840], P('dp', 'tensor')
- second_query: float32 [768, 3840], P('dp', 'tensor')
- next_keys: float32 [256, 5120], P('dp', 'tensor')
- moment_keys: float32 [256, 5120], P('dp', 'tensor')
- second_keys: float32 [256, 5120], P('dp', 'tensor')
- next_output: float32 [2560, 2560], P('tensor', 'dp')
- moment_output: float32 [2560, 2560], P('tensor', 'dp')
- second_output: float32 [2560, 2560], P('tensor', 'dp')
- next_gate: float32 [2560, 6400], P('dp', 'tensor')
- moment_gate: float32 [2560, 6400], P('dp', 'tensor')
- second_gate: float32 [2560, 6400], P('dp', 'tensor')
- next_up: float32 [2560, 6400], P('dp', 'tensor')
- moment_up: float32 [2560, 6400], P('dp', 'tensor')
- second_up: float32 [2560, 6400], P('dp', 'tensor')
- next_down: float32 [6400, 2560], P('tensor', 'dp')
- moment_down: float32 [6400, 2560], P('tensor', 'dp')
- second_down: float32 [6400, 2560], P('tensor', 'dp')
All inputs are finite; a program needn't handle non-finite values.
Results may differ from a plain program's by a relative error of at most 0.035.
Values may be sent and summed in bfloat16 or wider, within the bound.
No kernel may reach another device: no remote copies, remote signals or barrier semaphores. Data moves between devices by JAX's collectives and lax.ppermute only.
A program may use at most 192 MiB of HBM per device.

v0:
```python
import math

import jax
import jax.numpy as jnp
from jax import lax
from jax.sharding import PartitionSpec as P

D = 2560
HEADS = 40
NOPE = 64
ROPE = 32
VDIM = 64
QR = 768
KVR = 256
FF = 6400
ATT_ROWS = 512
STEP = 10


EPS = 1e-05
RESIDUAL = 1.4 / math.sqrt(62.0)
BETA_ONE = 0.9
BETA_TWO = 0.95
ADAM_EPS = 1e-08


def to_low(values):
    return values.astype(jnp.bfloat16)


def rotate(values, cosine, sine):
    half = values.shape[-1] // 2
    first = values[..., :half]
    second = values[..., half:]
    return jnp.concatenate(
        [first * cosine - second * sine, second * cosine + first * sine], axis=-1
    )


def unrotate(grads, cosine, sine):
    half = grads.shape[-1] // 2
    first = grads[..., :half]
    second = grads[..., half:]
    return jnp.concatenate(
        [first * cosine + second * sine, second * cosine - first * sine], axis=-1
    )


def tables(positions):
    half = ROPE // 2
    freqs = 10000.0 ** (-jnp.arange(half, dtype=jnp.float32) * 2.0 / ROPE)
    angles = positions[:, None] * freqs[None, :]
    return (jnp.cos(angles), jnp.sin(angles))


def rms_forward(values, gain):
    factor = lax.rsqrt(jnp.mean(values * values, axis=-1, keepdims=True) + EPS)
    return (values * factor * gain, factor)


def rms_backward(grad_out, values, factor, gain):
    scaled = grad_out * gain
    width = values.shape[-1]
    inner = jnp.sum(scaled * values, axis=-1, keepdims=True) / width
    grad_in = factor * scaled - values * factor * factor * factor * inner
    grad_gain = jnp.sum(grad_out * values * factor, axis=0)
    return (grad_in, grad_gain)


def block_scores(block_queries, keys_part, begin, key_pos, scale):
    logits = (
        jnp.einsum("qhd,khd->hqk", block_queries, keys_part, preferred_element_type=jnp.float32)
        * scale
    )
    rows_here = begin + jnp.arange(block_queries.shape[0])
    return jnp.where((rows_here[:, None] >= key_pos[None, :])[None], logits, -1e30)


def adamw(weight, grad, moment, second, rate, decay):
    moment_new = BETA_ONE * moment + (1.0 - BETA_ONE) * grad
    second_new = BETA_TWO * second + (1.0 - BETA_TWO) * grad * grad
    corr_one = 1.0 - BETA_ONE**STEP
    corr_two = 1.0 - BETA_TWO**STEP
    stepped = moment_new / corr_one / (jnp.sqrt(second_new / corr_two) + ADAM_EPS)
    return (weight - rate * (stepped + decay * weight), moment_new, second_new)


def rate_table():
    return (
        2.0,
        3.0 / math.sqrt(D),
        3.0 / math.sqrt(QR),
        3.0 / math.sqrt(KVR),
        3.0 / math.sqrt(HEADS * VDIM // 256),
        3.0 / math.sqrt(D),
        3.0 / math.sqrt(D),
        3.0 / math.sqrt(FF // 64),
    )


def shards(
    block_input,
    out_grad,
    norm_gains,
    latent_weight,
    query_weight,
    keys_weight,
    output_weight,
    gate_weight,
    up_weight,
    down_weight,
    gains_moment,
    gains_second,
    latent_moment,
    latent_second,
    query_moment,
    query_second,
    keys_moment,
    keys_second,
    output_moment,
    output_second,
    gate_moment,
    gate_second,
    up_moment,
    up_second,
    down_moment,
    down_second,
):
    tok_rows = block_input.shape[0]
    seq_rows = tok_rows * lax.axis_size("tensor")
    heads_here = output_weight.shape[0] // VDIM
    head_width = NOPE + ROPE
    pair_width = NOPE + VDIM
    scale = 1.0 / math.sqrt(head_width)
    gains_low, latent_full = (
        lax.all_gather(to_low(norm_gains), ("dp", "tensor"), axis=0, tiled=True),
        lax.all_gather(to_low(latent_weight), ("dp", "tensor"), axis=0, tiled=True),
    )
    gains_all = gains_low.astype(jnp.float32)
    gain_one = gains_all[:D]
    gain_two = gains_all[D : 2 * D]
    gain_query = gains_all[2 * D : 2 * D + QR]
    gain_keys = gains_all[2 * D + QR :]
    query_full, keys_matrix, output_full = (
        lax.all_gather(to_low(query_weight), "dp", axis=0, tiled=True),
        lax.all_gather(to_low(keys_weight), "dp", axis=0, tiled=True),
        lax.all_gather(to_low(output_weight), "dp", axis=1, tiled=True),
    )
    own_pos = (lax.axis_index("tensor") * tok_rows + jnp.arange(tok_rows)).astype(jnp.float32)
    own_cos, own_sin = tables(own_pos)
    tokens = block_input.astype(jnp.float32)
    normed_pre, factor_one = rms_forward(tokens, gain_one)
    normed = to_low(normed_pre)
    latent = jnp.dot(normed, latent_full, preferred_element_type=jnp.float32)
    query_part = latent[:, :QR]
    keys_part = latent[:, QR : QR + KVR]
    query_pre, factor_query = rms_forward(query_part, gain_query)
    keys_pre, factor_keys = rms_forward(keys_part, gain_keys)
    packed = jnp.concatenate(
        [
            to_low(query_pre),
            to_low(keys_pre),
            to_low(rotate(latent[:, QR + KVR :], own_cos, own_sin)),
        ],
        axis=1,
    )
    gathered = lax.all_gather(packed, "tensor", axis=0, tiled=True)
    query_lat = gathered[:, :QR]
    keys_lat = gathered[:, QR : QR + KVR]
    shared_rot = gathered[:, QR + KVR :]
    cosine, sine = tables(jnp.arange(seq_rows, dtype=jnp.float32))
    head_cos = cosine[:, None, :]
    head_sin = sine[:, None, :]
    query_raw = jnp.dot(query_lat, query_full, preferred_element_type=jnp.float32).reshape(
        seq_rows, heads_here, head_width
    )
    queries = to_low(
        jnp.concatenate(
            [query_raw[..., :NOPE], rotate(query_raw[..., NOPE:], head_cos, head_sin)], axis=-1
        )
    )
    keys_raw = jnp.dot(keys_lat, keys_matrix, preferred_element_type=jnp.float32).reshape(
        seq_rows, heads_here, pair_width
    )
    keys_all = jnp.concatenate(
        [
            to_low(keys_raw[..., :NOPE]),
            jnp.broadcast_to(shared_rot[:, None, :], (seq_rows, heads_here, ROPE)),
        ],
        axis=-1,
    )
    values_all = to_low(keys_raw[..., NOPE:])
    key_pos = jnp.arange(seq_rows)
    blocks = seq_rows // ATT_ROWS
    attended_parts = []
    lse_parts = []
    for block_index in range(blocks):
        begin = block_index * ATT_ROWS
        finish = begin + ATT_ROWS
        logits = block_scores(
            queries[begin:finish], keys_all[:finish], begin, key_pos[:finish], scale
        )
        peak = jnp.max(logits, axis=-1, keepdims=True)
        expo = jnp.exp(logits - peak)
        totals = jnp.sum(expo, axis=-1, keepdims=True)
        probs = to_low(expo / totals)
        lse_parts.append(peak + jnp.log(totals))
        attended_parts.append(
            to_low(
                jnp.einsum(
                    "hqk,khd->qhd", probs, values_all[:finish], preferred_element_type=jnp.float32
                )
            )
        )
    attended = jnp.concatenate(attended_parts, axis=0).reshape(seq_rows, heads_here * VDIM)
    branch = lax.psum_scatter(
        jnp.dot(attended, output_full, preferred_element_type=jnp.float32).astype(jnp.bfloat16),
        "tensor",
        scatter_dimension=0,
        tiled=True,
    ).astype(jnp.float32)
    hidden_state = tokens + RESIDUAL * branch
    mlp_pre, factor_two = rms_forward(hidden_state, gain_two)
    gate_full, upper_full, down_full = (
        lax.all_gather(to_low(gate_weight), "dp", axis=0, tiled=True),
        lax.all_gather(to_low(up_weight), "dp", axis=0, tiled=True),
        lax.all_gather(to_low(down_weight), "dp", axis=1, tiled=True),
    )
    mlp_in_all, cot_all = (
        lax.all_gather(to_low(mlp_pre), "tensor", axis=0, tiled=True),
        lax.all_gather(out_grad, "tensor", axis=0, tiled=True),
    )
    gate = jnp.dot(mlp_in_all, gate_full, preferred_element_type=jnp.float32)
    upper = jnp.dot(mlp_in_all, upper_full, preferred_element_type=jnp.float32)
    sigma = jax.nn.sigmoid(gate)
    hidden = to_low(gate * sigma * upper)
    mlp_out = lax.psum_scatter(
        jnp.dot(hidden, down_full, preferred_element_type=jnp.float32).astype(jnp.bfloat16),
        "tensor",
        scatter_dimension=0,
        tiled=True,
    ).astype(jnp.float32)
    block_output = hidden_state + RESIDUAL * mlp_out
    down_cot = to_low(RESIDUAL * cot_all.astype(jnp.float32))
    grad_hidden = jnp.einsum("sd,fd->sf", down_cot, down_full, preferred_element_type=jnp.float32)
    grad_gate_low = to_low(grad_hidden * upper * sigma * (1.0 + gate * (1.0 - sigma)))
    grad_up_low = to_low(grad_hidden * gate * sigma)
    grad_mlp_in = lax.psum_scatter(
        (
            jnp.einsum("sf,df->sd", grad_gate_low, gate_full, preferred_element_type=jnp.float32)
            + jnp.einsum("sf,df->sd", grad_up_low, upper_full, preferred_element_type=jnp.float32)
        ).astype(jnp.bfloat16),
        "tensor",
        scatter_dimension=0,
        tiled=True,
    ).astype(jnp.float32)
    grad_down = jnp.einsum("sf,sd->fd", hidden, down_cot, preferred_element_type=jnp.float32)
    grad_gate_w = jnp.einsum(
        "sd,sf->df", mlp_in_all, grad_gate_low, preferred_element_type=jnp.float32
    )
    grad_up_w = jnp.einsum("sd,sf->df", mlp_in_all, grad_up_low, preferred_element_type=jnp.float32)
    mlp_sums = (
        lax.psum_scatter(
            grad_gate_w.astype(jnp.bfloat16), "dp", scatter_dimension=0, tiled=True
        ).astype(jnp.float32),
        lax.psum_scatter(
            grad_up_w.astype(jnp.bfloat16), "dp", scatter_dimension=0, tiled=True
        ).astype(jnp.float32),
        lax.psum_scatter(
            grad_down.astype(jnp.bfloat16), "dp", scatter_dimension=1, tiled=True
        ).astype(jnp.float32),
    )
    grad_norm_two, grad_gain_two = rms_backward(grad_mlp_in, hidden_state, factor_two, gain_two)
    grad_state = out_grad.astype(jnp.float32) + grad_norm_two
    branch_cot = to_low(RESIDUAL * grad_state)
    branch_cot_all = lax.all_gather(branch_cot, "tensor", axis=0, tiled=True)
    grad_output_w = jnp.einsum(
        "sa,sd->ad", attended, branch_cot_all, preferred_element_type=jnp.float32
    )
    grad_attended = to_low(
        jnp.einsum("sd,ad->sa", branch_cot_all, output_full, preferred_element_type=jnp.float32)
    ).reshape(seq_rows, heads_here, VDIM)
    grad_query_parts = []
    grad_keys = jnp.zeros((seq_rows, heads_here, head_width), jnp.float32)
    grad_values = jnp.zeros((seq_rows, heads_here, VDIM), jnp.float32)
    for block_index in range(blocks):
        begin = block_index * ATT_ROWS
        finish = begin + ATT_ROWS
        block_queries = queries[begin:finish]
        block_grad = grad_attended[begin:finish]
        keys_seen = keys_all[:finish]
        logits = block_scores(block_queries, keys_seen, begin, key_pos[:finish], scale)
        probs_full = jnp.exp(logits - lse_parts[block_index])
        grad_probs = jnp.einsum(
            "qhd,khd->hqk", block_grad, values_all[:finish], preferred_element_type=jnp.float32
        )
        inner = jnp.sum(probs_full * grad_probs, axis=-1, keepdims=True)
        grad_logits = to_low(probs_full * (grad_probs - inner))
        grad_query_parts.append(
            jnp.einsum("hqk,khd->qhd", grad_logits, keys_seen, preferred_element_type=jnp.float32)
            * scale
        )
        grad_keys = grad_keys.at[:finish].add(
            jnp.einsum(
                "hqk,qhd->khd", grad_logits, block_queries, preferred_element_type=jnp.float32
            )
            * scale
        )
        grad_values = grad_values.at[:finish].add(
            jnp.einsum(
                "hqk,qhd->khd", to_low(probs_full), block_grad, preferred_element_type=jnp.float32
            )
        )
    grad_queries = jnp.concatenate(grad_query_parts, axis=0)
    grad_query_raw = to_low(
        jnp.concatenate(
            [grad_queries[..., :NOPE], unrotate(grad_queries[..., NOPE:], head_cos, head_sin)],
            axis=-1,
        )
    ).reshape(seq_rows, heads_here * head_width)
    grad_keys_raw = to_low(jnp.concatenate([grad_keys[..., :NOPE], grad_values], axis=-1)).reshape(
        seq_rows, heads_here * pair_width
    )
    grad_shared = jnp.sum(grad_keys[..., NOPE:], axis=1)
    grad_query_w = jnp.einsum(
        "sr,sc->rc", query_lat, grad_query_raw, preferred_element_type=jnp.float32
    )
    grad_keys_w = jnp.einsum(
        "sr,sc->rc", keys_lat, grad_keys_raw, preferred_element_type=jnp.float32
    )
    grad_latent_in = lax.psum_scatter(
        jnp.concatenate(
            [
                jnp.einsum(
                    "sc,rc->sr", grad_query_raw, query_full, preferred_element_type=jnp.float32
                ),
                jnp.einsum(
                    "sc,rc->sr", grad_keys_raw, keys_matrix, preferred_element_type=jnp.float32
                ),
                grad_shared,
            ],
            axis=1,
        ).astype(jnp.bfloat16),
        "tensor",
        scatter_dimension=0,
        tiled=True,
    ).astype(jnp.float32)
    attn_sums = (
        lax.psum_scatter(
            grad_query_w.astype(jnp.bfloat16), "dp", scatter_dimension=0, tiled=True
        ).astype(jnp.float32),
        lax.psum_scatter(
            grad_keys_w.astype(jnp.bfloat16), "dp", scatter_dimension=0, tiled=True
        ).astype(jnp.float32),
        lax.psum_scatter(
            grad_output_w.astype(jnp.bfloat16), "dp", scatter_dimension=1, tiled=True
        ).astype(jnp.float32),
    )
    grad_query_pre, grad_gain_query = rms_backward(
        grad_latent_in[:, :QR], query_part, factor_query, gain_query
    )
    grad_keys_pre, grad_gain_keys = rms_backward(
        grad_latent_in[:, QR : QR + KVR], keys_part, factor_keys, gain_keys
    )
    grad_rope = unrotate(grad_latent_in[:, QR + KVR :], own_cos, own_sin)
    grad_latent = to_low(jnp.concatenate([grad_query_pre, grad_keys_pre, grad_rope], axis=1))
    grad_latent_w = jnp.einsum("sd,sc->dc", normed, grad_latent, preferred_element_type=jnp.float32)
    grad_normed = jnp.einsum(
        "sc,dc->sd", grad_latent, latent_full, preferred_element_type=jnp.float32
    )
    grad_norm_one, grad_gain_one = rms_backward(grad_normed, tokens, factor_one, gain_one)
    input_grad = grad_state + grad_norm_one
    grad_gains = jnp.concatenate([grad_gain_one, grad_gain_two, grad_gain_query, grad_gain_keys])
    shared_sums = (
        lax.psum_scatter(grad_latent_w, ("dp", "tensor"), scatter_dimension=0, tiled=True),
        lax.psum_scatter(grad_gains, ("dp", "tensor"), scatter_dimension=0, tiled=True),
    )
    rates = rate_table()
    next_gains, moment_gains, second_gains = adamw(
        norm_gains, shared_sums[1], gains_moment, gains_second, rates[0], 0.0
    )
    next_latent, moment_latent, second_latent = adamw(
        latent_weight, shared_sums[0], latent_moment, latent_second, rates[1], 0.1
    )
    next_query, moment_query, second_query = adamw(
        query_weight, attn_sums[0], query_moment, query_second, rates[2], 0.1
    )
    next_keys, moment_keys, second_keys = adamw(
        keys_weight, attn_sums[1], keys_moment, keys_second, rates[3], 0.1
    )
    next_output, moment_output, second_output = adamw(
        output_weight, attn_sums[2], output_moment, output_second, rates[4], 0.1
    )
    next_gate, moment_gate, second_gate = adamw(
        gate_weight, mlp_sums[0], gate_moment, gate_second, rates[5], 0.1
    )
    next_up, moment_up, second_up = adamw(
        up_weight, mlp_sums[1], up_moment, up_second, rates[6], 0.1
    )
    next_down, moment_down, second_down = adamw(
        down_weight, mlp_sums[2], down_moment, down_second, rates[7], 0.1
    )
    return (
        block_output,
        input_grad,
        next_gains,
        moment_gains,
        second_gains,
        next_latent,
        moment_latent,
        second_latent,
        next_query,
        moment_query,
        second_query,
        next_keys,
        moment_keys,
        second_keys,
        next_output,
        moment_output,
        second_output,
        next_gate,
        moment_gate,
        second_gate,
        next_up,
        moment_up,
        second_up,
        next_down,
        moment_down,
        second_down,
    )


def solution(mesh):
    placed = (
        P(("dp", "tensor"), None),
        P(("dp", "tensor"), None),
        P(("dp", "tensor")),
        P(("dp", "tensor"), None),
        P("dp", "tensor"),
        P("dp", "tensor"),
        P("tensor", "dp"),
        P("dp", "tensor"),
        P("dp", "tensor"),
        P("tensor", "dp"),
        P(("dp", "tensor")),
        P(("dp", "tensor")),
        P(("dp", "tensor"), None),
        P(("dp", "tensor"), None),
        P("dp", "tensor"),
        P("dp", "tensor"),
        P("dp", "tensor"),
        P("dp", "tensor"),
        P("tensor", "dp"),
        P("tensor", "dp"),
        P("dp", "tensor"),
        P("dp", "tensor"),
        P("dp", "tensor"),
        P("dp", "tensor"),
        P("tensor", "dp"),
        P("tensor", "dp"),
    )
    return jax.shard_map(
        shards,
        mesh=mesh,
        in_specs=placed,
        out_specs=(
            P(("dp", "tensor"), None),
            P(("dp", "tensor"), None),
            P(("dp", "tensor")),
            P(("dp", "tensor")),
            P(("dp", "tensor")),
            P(("dp", "tensor"), None),
            P(("dp", "tensor"), None),
            P(("dp", "tensor"), None),
            P("dp", "tensor"),
            P("dp", "tensor"),
            P("dp", "tensor"),
            P("dp", "tensor"),
            P("dp", "tensor"),
            P("dp", "tensor"),
            P("tensor", "dp"),
            P("tensor", "dp"),
            P("tensor", "dp"),
            P("dp", "tensor"),
            P("dp", "tensor"),
            P("dp", "tensor"),
            P("dp", "tensor"),
            P("dp", "tensor"),
            P("dp", "tensor"),
            P("tensor", "dp"),
            P("tensor", "dp"),
            P("tensor", "dp"),
        ),
        check_vma=False,
    )
```

profile of v0, /device:TPU:5, one launch (start us, length us, event | category | flops | bytes accessed | tf_op | source)
XLA Modules:
  0.0 1790.8 jit_solution(5809687040606754032)
XLA Ops:
  9.7 66.9 %all-reduce.2 = bf16[6144]{0:T(1024)(128)(2,1)S(1)} all-reduce(bf16[6144]{0:T(1024)(128)(2,1)S(1)} %dynamic-update-slice.10), channel_id=1, replica_groups=mesh['dp'=16,'tensor'=8] {'dp','tensor'}, use_global_device_ids=true, to_apply=%add.2 | all-reduce | flops 6144 | bytes 24576
  78.0 246.0 %all-gather.27.cloned.1.call-done = bf16[128,20,1056]{2,1,0:T(8,128)(2,1)} async-done(((bf16[1,20,1056]{2,1,0:T(8,128)(2,1)}), bf16[128,20,1056]{2,1,0:T(8,128)(2,1)}) %all-gather.27.cloned.1.call-update) | async-done | bytes 5406736 | tf_op jit(solution)/shard_map/all_gather | solution.py:137
  324.1 10.2 reshape.365
  342.5 17.0 all_gather.39
  360.6 18.7 %all_gather.40 = bf16[768,480]{1,0:T(8,128)(2,1)S(1)} all-gather(bf16[48,480]{1,0:T(8,128)(2,1)S(1)} %convert_element_type.185), channel_id=1, replica_groups=mesh['dp'=16,'tensor'=8] {'dp'}, dimensions={0}, use_global_device_ids=true | all-gather | bytes 783360 | tf_op jit(solution)/shard_map/all_gather | solution.py:145
  379.3 17.4 all-gather.11.cloned.1.call-done
  410.4 20.0 %all-gather.13.cloned.1.call-done = bf16[320,2560]{0,1:T(8,128)(2,1)} async-done(((bf16[320,160]{0,1:T(8,128)(2,1)}), bf16[320,2560]{0,1:T(8,128)(2,1)}) %all-gather.13.cloned.1.call-update) | async-done | bytes 1638416 | tf_op jit(solution)/shard_map/all_gather | solution.py:147
  438.5 89.3 %reduce-scatter.13.cloned.1.call-done = bf16[128,2560]{1,0:T(8,128)(2,1)} async-done(((bf16[1024,2560]{1,0:T(8,128)(2,1)}), bf16[128,2560]{1,0:T(8,128)(2,1)}) %reduce-scatter.13.cloned.1.call-update) | async-done | bytes 655376 | tf_op jit(solution)/shard_map/reduce_scatter | solution.py:216
  534.4 32.4 %all-gather.19.cloned.1.call-done = bf16[2560,800]{1,0:T(8,128)(2,1)} async-done(((bf16[160,800]{1,0:T(8,128)(2,1)}), bf16[2560,800]{1,0:T(8,128)(2,1)}) %all-gather.19.cloned.1.call-update) | async-done | bytes 4096016 | tf_op jit(solution)/shard_map/all_gather | solution.py:226
  566.8 82.6 %all-gather.15.cloned.1.call-done = bf16[1024,2560]{1,0:T(8,128)(2,1)} async-done(((bf16[128,2560]{1,0:T(8,128)(2,1)}), bf16[1024,2560]{1,0:T(8,128)(2,1)}) %all-gather.15.cloned.1.call-update) | async-done | bytes 5242896 | tf_op jit(solution)/shard_map/all_gather | solution.py:230
  649.4 10.0 fusion.132
  659.4 27.9 %all-gather.17.cloned.1.call-done = bf16[2560,800]{1,0:T(8,128)(2,1)} async-done(((bf16[160,800]{1,0:T(8,128)(2,1)}), bf16[2560,800]{1,0:T(8,128)(2,1)}) %all-gather.17.cloned.1.call-update) | async-done | bytes 4096016 | tf_op jit(solution)/shard_map/all_gather | solution.py:225
  687.4 10.0 fusion.131
  697.3 30.3 %all-gather.21.cloned.1.call-done = bf16[800,2560]{0,1:T(8,128)(2,1)} async-done(((bf16[800,160]{0,1:T(8,128)(2,1)}), bf16[800,2560]{0,1:T(8,128)(2,1)}) %all-gather.21.cloned.1.call-update) | async-done | bytes 4096016 | tf_op jit(solution)/shard_map/all_gather | solution.py:227
  727.6 82.7 %all-gather.23.cloned.1.call-done = bf16[1024,2560]{1,0:T(8,128)(2,1)} async-done(((bf16[128,2560]{1,0:T(8,128)(2,1)}), bf16[1024,2560]{1,0:T(8,128)(2,1)}) %all-gather.23.cloned.1.call-update) | async-done | bytes 5242896 | tf_op jit(solution)/shard_map/all_gather | solution.py:231
  810.4 13.2 multiply_convert_fusion.5
  829.2 9.8 add_convert_fusion
  839.2 88.9 %reduce-scatter.17.cloned.1.call-done = bf16[128,2560]{1,0:T(8,128)(2,1)} async-done(((bf16[1024,2560]{1,0:T(8,128)(2,1)}), bf16[128,2560]{1,0:T(8,128)(2,1)}) %reduce-scatter.17.cloned.1.call-update) | async-done | bytes 655376 | tf_op jit(solution)/shard_map/reduce_scatter | solution.py:248
  932.9 78.9 %all-gather.25.cloned.1.call-done = bf16[1024,2560]{1,0:T(8,128)(2,1)} async-done(((bf16[128,2560]{1,0:T(8,128)(2,1)}), bf16[1024,2560]{1,0:T(8,128)(2,1)}) %all-gather.25.cloned.1.call-update) | async-done | bytes 5242896 | tf_op jit(solution)/shard_map/all_gather | solution.py:276
  1059.6 10.0 convolution_convert_fusion.3
  1071.1 9.8 convolution_convert_fusion.4
  1095.3 9.8 convolution_convert_fusion.1
  1105.2 17.3 reduce-scatter.31.cloned.1.call-done
  1131.3 55.8 %reduce-scatter.29.cloned.1.call-done = bf16[800,160]{0,1:T(8,128)(2,1)} async-done(((bf16[800,2560]{0,1:T(8,128)(2,1)}), bf16[800,160]{0,1:T(8,128)(2,1)}) %reduce-scatter.29.cloned.1.call-update) | async-done | bytes 256016 | tf_op jit(solution)/shard_map/reduce_scatter | solution.py:269
  1189.8 65.9 %reduce-scatter.27.cloned.1.call-done = bf16[160,800]{1,0:T(8,128)(2,1)} async-done(((bf16[2560,800]{1,0:T(8,128)(2,1)}), bf16[160,800]{1,0:T(8,128)(2,1)}) %reduce-scatter.27.cloned.1.call-update) | async-done | bytes 256016 | tf_op jit(solution)/shard_map/reduce_scatter | solution.py:266
  1258.5 65.6 %reduce-scatter.25.cloned.1.call-done = bf16[160,800]{1,0:T(8,128)(2,1)} async-done(((bf16[2560,800]{1,0:T(8,128)(2,1)}), bf16[160,800]{1,0:T(8,128)(2,1)}) %reduce-scatter.25.cloned.1.call-update) | async-done | bytes 256016 | tf_op jit(solution)/shard_map/reduce_scatter | solution.py:263
  1326.7 58.8 %reduce-scatter.21.cloned.1.call-done = bf16[16,640]{1,0:T(8,128)(2,1)} async-done(((bf16[256,640]{1,0:T(8,128)(2,1)}), bf16[16,640]{1,0:T(8,128)(2,1)}) %reduce-scatter.21.cloned.1.call-update) | async-done | bytes 20496 | tf_op jit(solution)/shard_map/reduce_scatter | solution.py:352
  1387.0 61.1 %reduce-scatter.19.cloned.1.call-done = bf16[48,480]{1,0:T(8,128)(2,1)} async-done(((bf16[768,480]{1,0:T(8,128)(2,1)}), bf16[48,480]{1,0:T(8,128)(2,1)}) %reduce-scatter.19.cloned.1.call-update) | async-done | bytes 46096 | tf_op jit(solution)/shard_map/reduce_scatter | solution.py:349
  1449.7 62.1 %reduce-scatter.23.cloned.1.call-done = bf16[320,160]{0,1:T(8,128)(2,1)} async-done(((bf16[320,2560]{0,1:T(8,128)(2,1)}), bf16[320,160]{0,1:T(8,128)(2,1)}) %reduce-scatter.23.cloned.1.call-update) | async-done | bytes 102416 | tf_op jit(solution)/shard_map/reduce_scatter | solution.py:355
  1519.8 72.3 %all-reduce.3 = f32[6144]{0:T(1024)S(1)} all-reduce(f32[6144]{0:T(1024)S(1)} %pad_maximum_fusion.16), channel_id=6, replica_groups=mesh['dp'=16,'tensor'=8] {'dp','tensor'}, use_global_device_ids=true, to_apply=%region_23.24.clone | all-reduce | flops 6144 | bytes 49152
  1592.7 18.2 %reduce-scatter.15.cloned.1.call-done = bf16[128,2560]{1,0:T(8,128)(2,1)} async-done(((bf16[1024,2560]{1,0:T(8,128)(2,1)}), bf16[128,2560]{1,0:T(8,128)(2,1)}) %reduce-scatter.15.cloned.1.call-update) | async-done | bytes 655376 | tf_op jit(solution)/shard_map/reduce_scatter | solution.py:237
  1615.1 166.9 %all-reduce.7.cloned.1.call-done = f32[2560,1056]{1,0:T(8,128)} async-done(((f32[2560,1056]{1,0:T(8,128)}), f32[2560,1056]{1,0:T(8,128)}) %all-reduce.7.cloned.1.call-update) | async-done | bytes 10813456
  (313 shorter events, 149.2 us)
Async XLA Ops:
  7.2 316.9 %all-gather.27.cloned.1.call-start = ((), (), s32[]{:S(2)}) async-start(), calls=%async_computation.27 | async-start | bytes 7133184 | tf_op jit(solution)/shard_map/all_gather | solution.py:137
  8.8 387.9 %all-gather.11.cloned.1.call-start = ((), (), s32[]{:S(2)}) async-start(), calls=%async_computation.10 | async-start | bytes 2433024 | tf_op jit(solution)/shard_map/all_gather | solution.py:167
  76.6 263.2 %copy-start.52 = (f32[256]{0:T(256)}, f32[256]{0:T(256)S(1)}, u32[]{:S(2)}) copy-start(f32[256]{0:T(256)S(1)} %slice.243) | copy-start | bytes 3076
  76.6 263.3 %copy-start.49 = (f32[768]{0:T(1024)}, f32[768]{0:T(1024)S(1)}, u32[]{:S(2)}) copy-start(f32[768]{0:T(1024)S(1)} %slice.241) | copy-start | bytes 9220
  76.6 265.3 %copy-start.60 = (f32[16]{0:T(128)}, f32[16]{0:T(128)S(1)}, u32[]{:S(2)}) copy-start(f32[16]{0:T(128)S(1)} %multiply_power_fusion) | copy-start | bytes 196
  76.6 262.9 %copy-start.67 = (f32[128]{0:T(128)}, f32[128]{0:T(128)S(1)}, u32[]{:S(2)}) copy-start(f32[128]{0:T(128)S(1)} %add_convert_fusion.3) | copy-start | bytes 1540
  78.0 256.3 %copy-start.54 = (f32[128]{0:T(128)}, f32[128]{0:T(128)S(1)}, u32[]{:S(2)}) copy-start(f32[128]{0:T(128)S(1)} %add_rsqrt_fusion.3) | copy-start | bytes 1540
  78.0 256.2 %copy-start.40 = (f32[2560]{0:T(1024)}, f32[2560]{0:T(1024)S(1)}, u32[]{:S(2)}) copy-start(f32[2560]{0:T(1024)S(1)} %get-tuple-element.137) | copy-start | bytes 30724
  78.0 256.2 %copy-start.2 = (bf16[128,2560]{1,0:T(8,128)(2,1)S(1)}, bf16[128,2560]{1,0:T(8,128)(2,1)}, u32[]{:S(2)}) copy-start(bf16[128,2560]{1,0:T(8,128)(2,1)} %param.38) | copy-start | bytes 1966084
  341.1 89.3 %all-gather.13.cloned.1.call-start = ((), (), s32[]{:S(2)}) async-start(), calls=%async_computation.11 | async-start | bytes 2088960 | tf_op jit(solution)/shard_map/all_gather | solution.py:147
  341.8 186.0 %reduce-scatter.13.cloned.1.call-start = ((), (), s32[]{:S(2)}) async-start(), calls=%async_computation.12 | async-start | bytes 5898240 | tf_op jit(solution)/shard_map/reduce_scatter | solution.py:216
  436.7 130.2 %all-gather.19.cloned.1.call-start = ((), (), s32[]{:S(2)}) async-start(), calls=%async_computation.15 | async-start | bytes 4874240 | tf_op jit(solution)/shard_map/all_gather | solution.py:226
  438.5 210.9 %all-gather.15.cloned.1.call-start = ((), (), s32[]{:S(2)}) async-start(), calls=%async_computation.13 | async-start | bytes 5898240 | tf_op jit(solution)/shard_map/all_gather | solution.py:230
  529.3 400.5 %copy-start.56 = (f32[128]{0:T(128)}, f32[128]{0:T(128)S(1)}, u32[]{:S(2)}) copy-start(f32[128]{0:T(128)S(1)} %add_rsqrt_fusion) | copy-start | bytes 1540
  531.5 155.8 %all-gather.17.cloned.1.call-start = ((), (), s32[]{:S(2)}) async-start(), calls=%async_computation.14 | async-start | bytes 4874240 | tf_op jit(solution)/shard_map/all_gather | solution.py:225
  532.4 195.3 %all-gather.21.cloned.1.call-start = ((), (), s32[]{:S(2)}) async-start(), calls=%async_computation.16 | async-start | bytes 4874240 | tf_op jit(solution)/shard_map/all_gather | solution.py:227
  533.2 277.2 %all-gather.23.cloned.1.call-start = ((), (), s32[]{:S(2)}) async-start(), calls=%async_computation.18 | async-start | bytes 5898240 | tf_op jit(solution)/shard_map/all_gather | solution.py:231
  533.9 394.1 %reduce-scatter.17.cloned.1.call-start = ((), (), s32[]{:S(2)}) async-start(), calls=%async_computation.19 | async-start | bytes 5898240 | tf_op jit(solution)/shard_map/reduce_scatter | solution.py:248
  839.1 172.7 %all-gather.25.cloned.1.call-start = ((), (), s32[]{:S(2)}) async-start(), calls=%async_computation.20 | async-start | bytes 5898240 | tf_op jit(solution)/shard_map/all_gather | solution.py:276
  932.5 190.0 %reduce-scatter.31.cloned.1.call-start = ((), (), s32[]{:S(2)}) async-start(), calls=%async_computation.28 | async-start | bytes 2654208
  1048.6 138.5 %reduce-scatter.29.cloned.1.call-start = ((), (), s32[]{:S(2)}) async-start(), calls=%async_computation.26 | async-start | bytes 4874240 | tf_op jit(solution)/shard_map/reduce_scatter | solution.py:269
  1058.2 197.5 %reduce-scatter.27.cloned.1.call-start = ((), (), s32[]{:S(2)}) async-start(), calls=%async_computation.25 | async-start | bytes 4874240 | tf_op jit(solution)/shard_map/reduce_scatter | solution.py:266
  1069.6 254.5 %reduce-scatter.25.cloned.1.call-start = ((), (), s32[]{:S(2)}) async-start(), calls=%async_computation.24 | async-start | bytes 4874240 | tf_op jit(solution)/shard_map/reduce_scatter | solution.py:263
  1080.9 304.7 %reduce-scatter.21.cloned.1.call-start = ((), (), s32[]{:S(2)}) async-start(), calls=%async_computation.22 | async-start | bytes 348160 | tf_op jit(solution)/shard_map/reduce_scatter | solution.py:352
  1084.6 363.5 %reduce-scatter.19.cloned.1.call-start = ((), (), s32[]{:S(2)}) async-start(), calls=%async_computation.21 | async-start | bytes 835584 | tf_op jit(solution)/shard_map/reduce_scatter | solution.py:349
  1088.3 423.5 %reduce-scatter.23.cloned.1.call-start = ((), (), s32[]{:S(2)}) async-start(), calls=%async_computation.23 | async-start | bytes 2088960 | tf_op jit(solution)/shard_map/reduce_scatter | solution.py:355
  1095.2 515.7 %reduce-scatter.15.cloned.1.call-start = ((), (), s32[]{:S(2)}) async-start(), calls=%async_computation.17 | async-start | bytes 5898240 | tf_op jit(solution)/shard_map/reduce_scatter | solution.py:237
  1105.2 676.8 %all-reduce.7.cloned.1.call-start = ((), (), s32[]{:S(2)}) async-start(), calls=%async_computation.29 | async-start | bytes 23592960
  1258.4 189.6 %copy-start.39 = (f32[48,480]{1,0:T(8,128)S(1)}, f32[48,480]{1,0:T(8,128)}, u32[]{:S(2)}) copy-start(f32[48,480]{1,0:T(8,128)} %param.42) | copy-start | bytes 276484
  1258.4 189.7 %copy-start.48 = (f32[48,480]{1,0:T(8,128)S(1)}, f32[48,480]{1,0:T(8,128)}, u32[]{:S(2)}) copy-start(f32[48,480]{1,0:T(8,128)} %param.52) | copy-start | bytes 276484
  1258.4 253.4 %copy-start.28 = (f32[320,160]{0,1:T(8,128)S(1)}, f32[320,160]{0,1:T(8,128)}, u32[]{:S(2)}) copy-start(f32[320,160]{0,1:T(8,128)} %param.44) | copy-start | bytes 614404
  1258.4 253.4 %copy-start.43 = (f32[320,160]{0,1:T(8,128)S(1)}, f32[320,160]{0,1:T(8,128)}, u32[]{:S(2)}) copy-start(f32[320,160]{0,1:T(8,128)} %param.56) | copy-start | bytes 614404
  (71 other events, 2708.7 us)
Sparse Core Ops, SparseCore 0:
  10.3 313.6 all-gather.26
  341.2 55.4 all-gather.10
  399.0 31.3 all-gather.12
  436.8 91.0 reduce-scatter.12
  530.0 36.7 all-gather.18
  569.0 80.3 all-gather.14
  651.7 35.6 all-gather.16
  689.6 37.9 all-gather.20
  729.9 80.3 all-gather.22
  839.2 88.7 reduce-scatter.16
  932.6 79.1 all-gather.24
  1048.8 73.6 reduce-scatter.30
  1124.9 62.1 reduce-scatter.28
  1189.4 66.1 reduce-scatter.26
  1257.9 66.1 reduce-scatter.24
  1326.3 59.2 reduce-scatter.20
  1388.5 59.5 reduce-scatter.18
  1450.3 61.4 reduce-scatter.22
  1516.1 94.7 reduce-scatter.14
  1616.6 165.3 all-reduce.6
where the time goes:
time: 1800 us; the launch traced here: 1790 us
  waiting for transfers between devices  1370 us (76%)
  blocking collectives  175 us (10%)
  matrix products  158 us (9%)
  other arithmetic  46.2 us (3%)
  local copies, waits for them, and re-layouts  25 us (1%)
    all_gather x1, waiting for transfers between devices, shards(): lax.all_gather(to_low(latent_weight), ('dp', 'tensor'), axis=0, tiled=True)  246 us
    unnamed x22, waiting for transfers between devices  185 us
    unnamed x2, blocking collectives  139 us
    reduce_scatter x1, waiting for transfers between devices, shards(): lax.psum_scatter(jnp.dot(attended, output_full, preferred_element_type=jn...  89.3 us
    reduce_scatter x1, waiting for transfers between devices, shards(): lax.psum_scatter((jnp.einsum('sf,df->sd', grad_gate_low, gate_full, prefe...  88.9 us
    all_gather x1, waiting for transfers between devices, shards(): lax.all_gather(out_grad, 'tensor', axis=0, tiled=True)  82.7 us
    all_gather x1, waiting for transfers between devices, shards(): lax.all_gather(to_low(mlp_pre), 'tensor', axis=0, tiled=True)  82.6 us
    all_gather x1, waiting for transfers between devices, shards(): branch_cot_all = lax.all_gather(branch_cot, 'tensor', axis=0, tiled=True)  78.9 us
  transfers between devices with their start and end apart: 20, of which 20 were waited for; matrix products, arithmetic and copies ran while one was open for 7% of the time, Pallas kernels for 0%

commit v1 on v0

v1 whole, which is shorter than its diff:
```python
import math

import jax
import jax.numpy as jnp
from jax import lax
from jax.experimental import pallas as pl
from jax.experimental.pallas import tpu as pltpu
from jax.sharding import PartitionSpec as P

D = 2560
HEADS = 40
NOPE = 64
ROPE = 32
VDIM = 64
QR = 768
KVR = 256
FF = 6400
STEP = 10
RING = 4
SLICE = 320
LANES = 128
CELL = 256
BLOCK = 512
AXES = ("yl", "x", "c", "yh", "z")
SIZES = (2, 4, 2, 2, 4)
PLANE = ("yl", "x", "yh")


EPS = 1e-05
RESIDUAL = 1.4 / math.sqrt(62.0)
BETA_ONE = 0.9
BETA_TWO = 0.95
ADAM_EPS = 1e-08


def to_low(values):
    return values.astype(jnp.bfloat16)


def rotate(values, cosine, sine):
    half = values.shape[-1] // 2
    first = values[..., :half]
    second = values[..., half:]
    return jnp.concatenate(
        [first * cosine - second * sine, second * cosine + first * sine], axis=-1
    )


def unrotate(grads, cosine, sine):
    half = grads.shape[-1] // 2
    first = grads[..., :half]
    second = grads[..., half:]
    return jnp.concatenate(
        [first * cosine + second * sine, second * cosine - first * sine], axis=-1
    )


def tables(positions):
    half = ROPE // 2
    freqs = 10000.0 ** (-jnp.arange(half, dtype=jnp.float32) * 2.0 / ROPE)
    angles = positions[:, None] * freqs[None, :]
    return (jnp.cos(angles), jnp.sin(angles))


def rms_forward(values, gain):
    factor = lax.rsqrt(jnp.mean(values * values, axis=-1, keepdims=True) + EPS)
    return (values * factor * gain, factor)


def rms_backward(grad_out, values, factor, gain):
    scaled = grad_out * gain
    width = values.shape[-1]
    inner = jnp.sum(scaled * values, axis=-1, keepdims=True) / width
    grad_in = factor * scaled - values * factor * factor * factor * inner
    grad_gain = jnp.sum(grad_out * values * factor, axis=0)
    return (grad_in, grad_gain)


def adamw(weight, grad, moment, second, rate, decay):
    moment_new = BETA_ONE * moment + (1.0 - BETA_ONE) * grad
    second_new = BETA_TWO * second + (1.0 - BETA_TWO) * grad * grad
    corr_one = 1.0 - BETA_ONE**STEP
    corr_two = 1.0 - BETA_TWO**STEP
    stepped = moment_new / corr_one / (jnp.sqrt(second_new / corr_two) + ADAM_EPS)
    return (weight - rate * (stepped + decay * weight), moment_new, second_new)


def rate_table():
    return (
        2.0,
        3.0 / math.sqrt(D),
        3.0 / math.sqrt(QR),
        3.0 / math.sqrt(KVR),
        3.0 / math.sqrt(HEADS * VDIM // 256),
        3.0 / math.sqrt(D),
        3.0 / math.sqrt(D),
        3.0 / math.sqrt(FF // 64),
    )


def ring(step):
    return [(place, (place + step) % RING) for place in range(RING)]


def send_z(block, step):
    return lax.ppermute(block, "z", ring(step))


def send_x(block, step):
    return lax.ppermute(block, "x", ring(step))


def send_y(block, step):
    pairs = [(a % 2 * 2 + a // 2, b % 2 * 2 + b // 2) for a, b in ring(step)]
    return lax.ppermute(block, ("yl", "yh"), pairs)


def send_core(block):
    return lax.ppermute(block, "c", [(0, 1), (1, 0)])


def swap(block):
    return lax.ppermute(block, ("c", "yh"), [(0, 0), (1, 2), (2, 1), (3, 3)])


def pick(place, rel, index):
    return lax.select_n(place, *[rel[(own - index) % RING] for own in range(RING)])


def in_order(place, rel):
    return [pick(place, rel, index) for index in range(RING)]


def tie(keep, *others):
    anywhere = pl.BlockSpec(memory_space=pl.ANY)
    count = len(keep)
    return pl.pallas_call(
        lambda *refs: None,
        in_specs=[anywhere] * (count + len(others)),
        out_specs=[anywhere] * count,
        out_shape=[jax.ShapeDtypeStruct(array.shape, array.dtype) for array in keep],
        input_output_aliases={index: index for index in range(count)},
        name="tie",
    )(*keep, *others)


def gather_group(block):
    half = block.shape[0] // 2
    after, before = send_z(block, 1), send_z(block, -1)
    across = jnp.concatenate([send_z(after[:half], 1), send_z(before[half:], -1)], axis=0)
    return [(part, send_core(part)) for part in (block, after, across, before)]


def joined(pairs):
    return jnp.concatenate([part for pair in pairs for part in pair], axis=0)


def scatter_ring(sums):
    half = sums[0].shape[0] // 2
    across = to_low(sums[2])
    down = send_z(across[:half], -1).astype(jnp.float32)
    up = send_z(across[half:], 1).astype(jnp.float32)
    after = jnp.concatenate([sums[1][:half] + down, sums[1][half:]], axis=0)
    before = jnp.concatenate([sums[3][:half], sums[3][half:] + up], axis=0)
    return (
        sums[0]
        + send_z(to_low(after), -1).astype(jnp.float32)
        + send_z(to_low(before), 1).astype(jnp.float32)
    )


def scatter_group(pairs):
    return scatter_ring(
        [mine.astype(jnp.float32) + send_core(other).astype(jnp.float32) for mine, other in pairs]
    )


def scatter_halves(mine, other):
    rows = mine.shape[0] // RING
    sums = mine.astype(jnp.float32) + send_core(other).astype(jnp.float32)
    return scatter_ring([sums[rows * step : rows * (step + 1)] for step in range(RING)])


def to_abs(mine, other, place):
    mine = jnp.concatenate(in_order(place["z"], mine), axis=0)
    other = jnp.concatenate(in_order(place["z"], other), axis=0)
    first = place["c"] == 0
    return jnp.concatenate(
        [jnp.where(first, mine, other), jnp.where(first, other, mine)], axis=0
    )


def to_rel(rows, place):
    size = rows.shape[0] // (2 * RING)
    halves = []
    for core in (place["c"], 1 - place["c"]):
        spots = [(place["z"] - step) % RING for step in range(RING)]
        halves.append(
            jnp.concatenate(
                [
                    lax.dynamic_slice_in_dim(rows, (core * RING + spot) * size, size, axis=0)
                    for spot in spots
                ],
                axis=0,
            )
        )
    return halves


def empty(shape):
    return pl.pallas_call(
        lambda ref: None,
        out_specs=pl.BlockSpec(memory_space=pl.ANY),
        out_shape=jax.ShapeDtypeStruct(shape, jnp.bfloat16),
        name="empty",
    )()


def line_y(blocks):
    return [blocks[0], blocks[2], blocks[1], blocks[3]]


def spot_y(place, step):
    spot = (place["y"] + step) % RING
    return spot % 2 * 2 + spot // 2


def spot_x(place, step):
    return (place["x"] + step) % RING


def first_x(block, place):
    return jnp.stack(in_order(place["x"], [block] + [send_x(block, s) for s in (1, 2, 3)]))


def first_y(block, place):
    near = [block] + [send_y(block, s) for s in (1, 2, 3)]
    return jnp.stack(line_y(in_order(place["y"], near)))


def second(line, place, send, spot):
    half = line.shape[0] // 2
    after, before = send(line, 1), send(line, -1)
    across = jnp.concatenate([send(after[:half], 1), send(before[half:], -1)], axis=0)
    out = empty((RING,) + line.shape)
    zeros = (0,) * line.ndim
    for step, part in enumerate((line, after, across, before)):
        out = lax.dynamic_update_slice(out, part[None], (spot(place, -step),) + zeros)
    return out


def second_y(line, place):
    return second(line, place, send_y, spot_y)


def second_x(line, place):
    return second(line, place, send_x, spot_x)


def fold(blocks, place, send, spot):
    def at(step):
        return lax.dynamic_index_in_dim(blocks, spot(place, step), axis=0, keepdims=False)

    across, after, before = at(2), at(1), at(3)
    half = across.shape[0] // 2
    up = send(across[:half], 1).astype(jnp.float32)
    down = send(across[half:], -1).astype(jnp.float32)
    after = after.astype(jnp.float32)
    before = before.astype(jnp.float32)
    after = to_low(jnp.concatenate([after[:half] + up, after[half:]], axis=0))
    before = to_low(jnp.concatenate([before[:half], before[half:] + down], axis=0))
    parts = (at(0), send(after, 1), send(before, -1))
    return to_low(sum(part.astype(jnp.float32) for part in parts))


def fold_x(blocks, place):
    return fold(blocks, place, send_x, spot_x)


def fold_y(blocks, place):
    return fold(blocks, place, send_y, spot_y)


def routes(x_first):
    pairs = []
    for source in range(32):
        rest, at_yh = divmod(source, 2)
        rest, at_c = divmod(rest, 2)
        at_yl, at_x = divmod(rest, 4)
        row = at_yl * 8 + at_x * 2 + at_c
        if x_first:
            to_yl, to_yh, to_x = row // 8, row // 4 % 2, row % 4
        else:
            to_x, to_yl, to_yh = row // 4, row // 2 % 2, row % 2
        pairs.append((source, ((to_yl * 4 + to_x) * 2 + at_yh) * 2 + to_yh))
    return pairs


def trade(block, x_first):
    return lax.ppermute(block, ("yl", "x", "c", "yh"), routes(x_first))


def trade_back(block, x_first):
    back = [(target, source) for source, target in routes(x_first)]
    return lax.ppermute(block, ("yl", "x", "c", "yh"), back)


def by_four(blocks, names):
    return lax.all_to_all(blocks, names, split_axis=0, concat_axis=0, tiled=True)


def four_copies(block):
    return jnp.broadcast_to(block[None], (RING,) + block.shape)


def ff_kernel(*refs):
    parts, (grad_ref, weight_ref, rest_ref), backs = refs[:4], refs[4:7], refs[-8:-4]
    rows_ref, hidden_ref, both_ref, total = refs[-4:]
    step = pl.program_id(0)
    last = pl.num_programs(0) - 1
    size = parts[0].shape[0]

    @pl.when(step == 0)
    def _():
        for index, part in enumerate(parts):
            rows_ref[index * size : (index + 1) * size] = part[...]

    def columns(source, half):
        weight = source[...]
        both = jnp.dot(rows_ref[...], weight, preferred_element_type=jnp.float32)
        gate, upper = both[:, :half], both[:, half:]
        grad = grad_ref[:, :half]
        sigma = jax.nn.sigmoid(gate)
        hidden_ref[:, :half] = to_low(gate * sigma * upper)
        grads = jnp.concatenate(
            [
                to_low(grad * upper * sigma * (1.0 + gate * (1.0 - sigma))),
                to_low(grad * gate * sigma),
            ],
            axis=1,
        )
        both_ref[:, : 2 * half] = grads
        return lax.dot_general(
            grads, weight, (((1,), (1,)), ((), ())), preferred_element_type=jnp.float32
        )

    @pl.when(step == 0)
    def _():
        total[...] = columns(weight_ref, CELL)

    @pl.when((step > 0) & (step < last))
    def _():
        total[...] += columns(weight_ref, CELL)

    @pl.when(step == last)
    def _():
        result = total[...] + columns(rest_ref, CELL // 2)
        for index, back in enumerate(backs):
            back[...] = to_low(result[index * size : (index + 1) * size])


def feed_forward(parts, grad_hidden, weights, rest, held, spot):
    size, width = parts[0].shape
    rows, columns = 4 * size, weights.shape[1] + CELL
    steps = pl.cdiv(columns, 2 * CELL)
    count = 2 * RING * size
    whole = pl.BlockSpec((size, width), lambda j: (0, 0))
    anywhere = pl.BlockSpec(memory_space=pl.ANY)
    return pl.pallas_call(
        ff_kernel,
        grid=(steps,),
        in_specs=[whole] * 4
        + [
            pl.BlockSpec((rows, CELL), lambda j: (spot, j)),
            pl.BlockSpec((width, 2 * CELL), lambda j: (0, jnp.minimum(j, steps - 2))),
            pl.BlockSpec((width, CELL), lambda j: (0, 0)),
        ]
        + [anywhere] * len(held),
        out_specs=[whole] * 4
        + [
            pl.BlockSpec((rows, width), lambda j: (spot, 0)),
            pl.BlockSpec((rows, CELL), lambda j: (spot, j)),
            pl.BlockSpec((rows, 2 * CELL), lambda j: (spot, j)),
        ],
        out_shape=[jax.ShapeDtypeStruct((size, width), jnp.bfloat16)] * 4
        + [
            jax.ShapeDtypeStruct((count, width), jnp.bfloat16),
            jax.ShapeDtypeStruct((count, columns // 2), jnp.bfloat16),
            jax.ShapeDtypeStruct((count, columns), jnp.bfloat16),
        ],
        scratch_shapes=[pltpu.VMEM((rows, width), jnp.float32)],
        input_output_aliases={7 + index: 4 + index for index in range(len(held))},
        compiler_params=pltpu.CompilerParams(vmem_limit_bytes=48 << 20),
        cost_estimate=pl.CostEstimate(
            flops=4 * rows * width * columns,
            bytes_accessed=20 << 20,
            transcendentals=rows * columns // 2,
        ),
        name="feed_forward",
    )(*parts, grad_hidden, weights, rest, *held)


def mix(gate, upper):
    parts = []
    for begin in range(0, gate.shape[1], CELL):
        parts += [gate[:, begin : begin + CELL], upper[:, begin : begin + CELL]]
    return jnp.concatenate(parts, axis=1)


def unmix(both):
    sides = ([], [])
    count = both.shape[1] // 2
    for begin in range(0, count, CELL):
        half = min(CELL, count - begin)
        for index in (0, 1):
            spot = 2 * begin + index * half
            sides[index].append(both[:, spot : spot + half])
    return [jnp.concatenate(side, axis=1) for side in sides]


def scatter_plane(blocks):
    return add_up(exchange_plane(blocks))


def exchange_plane(blocks):
    return lax.all_to_all(blocks, PLANE, split_axis=0, concat_axis=0, tiled=True)


def add_up(terms):
    return to_low(jnp.sum(terms.astype(jnp.float32), axis=0))


def rope_slots(seq_rows):
    cosine, sine = tables(jnp.arange(seq_rows, dtype=jnp.float32))
    half = ROPE // 2
    one = jnp.ones((seq_rows, NOPE), jnp.float32)
    none = jnp.zeros((seq_rows, half), jnp.float32)
    plain = jnp.zeros((seq_rows, NOPE), jnp.float32)
    own = jnp.concatenate([one, cosine, cosine, none, none], axis=1)
    later = jnp.concatenate([plain, -sine, none, none, none], axis=1)
    earlier = jnp.concatenate([plain, none, sine, none, none], axis=1)
    return own, later, earlier


def turn(values, own, later, earlier):
    half = ROPE // 2
    return (
        values * own
        + pltpu.roll(values, LANES - half, 1) * later
        + pltpu.roll(values, half, 1) * earlier
    )


def attention_kernel(
    query_ref, keys_ref, wq_ref, wk_ref, own_ref, later_ref, earlier_ref, shared_ref,
    q_ref, k_ref, kv_ref, out_ref,
):
    seq_rows = query_ref.shape[0]
    heads = wq_ref.shape[1] // LANES
    scale = 1.0 / math.sqrt(NOPE + ROPE)
    lane = lax.broadcasted_iota(jnp.int32, (seq_rows, LANES), 1)
    rows = lax.broadcasted_iota(jnp.int32, (BLOCK, BLOCK), 0)
    cols = lax.broadcasted_iota(jnp.int32, (BLOCK, BLOCK), 1)
    query_raw = jnp.dot(query_ref[...], wq_ref[...], preferred_element_type=jnp.float32)
    keys_raw = jnp.dot(keys_ref[...], wk_ref[...], preferred_element_type=jnp.float32)
    for head in range(heads):
        slot = slice(head * LANES, (head + 1) * LANES)
        q = to_low(turn(query_raw[:, slot], own_ref[...], later_ref[...], earlier_ref[...]))
        kv = to_low(keys_raw[:, slot])
        k = jnp.where(lane < NOPE, kv, shared_ref[...])
        q_ref[:, slot] = q
        k_ref[:, slot] = k
        kv_ref[:, slot] = kv
        for begin in range(0, seq_rows, BLOCK):
            end = begin + BLOCK
            logits = (
                lax.dot_general(
                    q[begin:end], k[:end], (((1,), (1,)), ((), ())),
                    preferred_element_type=jnp.float32,
                )
                * scale
            )
            edge = jnp.where(rows >= cols, logits[:, begin:], -1e30)
            logits = jnp.concatenate([logits[:, :begin], edge], axis=1) if begin else edge
            peak = jnp.max(logits, axis=1, keepdims=True)
            expo = jnp.exp(logits - peak)
            probs = to_low(expo * (1.0 / jnp.sum(expo, axis=1, keepdims=True)))
            found = jnp.dot(probs, kv[:end], preferred_element_type=jnp.float32)
            out_ref[begin:end, head * VDIM : (head + 1) * VDIM] = to_low(found[:, NOPE:])


def attention(query_lat, keys_lat, wq, wk, factors, shared):
    seq_rows = query_lat.shape[0]
    heads = wq.shape[1] // LANES
    whole = pl.BlockSpec(memory_space=pltpu.VMEM)
    wide = jax.ShapeDtypeStruct((seq_rows, heads * LANES), jnp.bfloat16)
    pairs = heads * seq_rows * seq_rows
    return pl.pallas_call(
        attention_kernel,
        in_specs=[whole] * 8,
        out_specs=[whole] * 4,
        out_shape=[wide] * 3 + [jax.ShapeDtypeStruct((seq_rows, heads * VDIM), jnp.bfloat16)],
        compiler_params=pltpu.CompilerParams(vmem_limit_bytes=48 << 20),
        cost_estimate=pl.CostEstimate(
            flops=512 * pairs, bytes_accessed=8 << 20, transcendentals=pairs // 2
        ),
        name="attention",
    )(query_lat, keys_lat, wq, wk, *factors, shared)


def attention_back_kernel(
    q_ref, k_ref, kv_ref, grad_ref, own_ref, later_ref, earlier_ref,
    dq_ref, dkv_ref, shared_ref, key_total, value_total,
):
    seq_rows = q_ref.shape[0]
    heads = q_ref.shape[1] // LANES
    scale = 1.0 / math.sqrt(NOPE + ROPE)
    lane = lax.broadcasted_iota(jnp.int32, (seq_rows, LANES), 1)
    rows = lax.broadcasted_iota(jnp.int32, (BLOCK, BLOCK), 0)
    cols = lax.broadcasted_iota(jnp.int32, (BLOCK, BLOCK), 1)
    for head in range(heads):
        slot = slice(head * LANES, (head + 1) * LANES)
        q, k, kv = q_ref[:, slot], k_ref[:, slot], kv_ref[:, slot]
        grad = grad_ref[:, head * VDIM : (head + 1) * VDIM]
        grad = jnp.concatenate([jnp.zeros_like(grad), grad], axis=1)
        key_total[...] = jnp.zeros_like(key_total)
        value_total[...] = jnp.zeros_like(value_total)
        for begin in range(0, seq_rows, BLOCK):
            end = begin + BLOCK
            q_here, grad_here = q[begin:end], grad[begin:end]
            turned = (((1,), (1,)), ((), ()))
            logits = (
                lax.dot_general(k[:end], q_here, turned, preferred_element_type=jnp.float32)
                * scale
            )
            edge = jnp.where(cols >= rows, logits[begin:], -1e30)
            logits = jnp.concatenate([logits[:begin], edge], axis=0) if begin else edge
            peak = jnp.max(logits, axis=0, keepdims=True)
            expo = jnp.exp(logits - peak)
            probs = expo * (1.0 / jnp.sum(expo, axis=0, keepdims=True))
            grad_probs = lax.dot_general(
                kv[:end], grad_here, turned, preferred_element_type=jnp.float32
            )
            inner = jnp.sum(probs * grad_probs, axis=0, keepdims=True)
            grad_logits = to_low(probs * (grad_probs - inner))
            key_total[:end] += jnp.dot(grad_logits, q_here, preferred_element_type=jnp.float32)
            value_total[:end] += jnp.dot(
                to_low(probs), grad_here, preferred_element_type=jnp.float32
            )
            found = (
                lax.dot_general(
                    grad_logits, k[:end], (((0,), (0,)), ((), ())),
                    preferred_element_type=jnp.float32,
                )
                * scale
            )
            dq_ref[begin:end, slot] = to_low(
                turn(found, own_ref[begin:end], -later_ref[begin:end], -earlier_ref[begin:end])
            )
        keys = key_total[...] * scale
        dkv_ref[:, slot] = to_low(jnp.where(lane < NOPE, keys, value_total[...]))
        if head:
            shared_ref[...] += keys
        else:
            shared_ref[...] = keys


def attention_back(q, k, kv, grad, factors):
    seq_rows, width = q.shape
    whole = pl.BlockSpec(memory_space=pltpu.VMEM)
    wide = jax.ShapeDtypeStruct((seq_rows, width), jnp.bfloat16)
    pairs = width // LANES * seq_rows * seq_rows
    total = pltpu.VMEM((seq_rows, LANES), jnp.float32)
    return pl.pallas_call(
        attention_back_kernel,
        in_specs=[whole] * 7,
        out_specs=[whole] * 3,
        out_shape=[wide, wide, jax.ShapeDtypeStruct((seq_rows, LANES), jnp.float32)],
        scratch_shapes=[total, total],
        compiler_params=pltpu.CompilerParams(vmem_limit_bytes=48 << 20),
        cost_estimate=pl.CostEstimate(
            flops=1280 * pairs, bytes_accessed=10 << 20, transcendentals=pairs // 2
        ),
        name="attention_back",
    )(q, k, kv, grad, *factors)


def to_slots(weight):
    rows = weight.shape[0]
    return jnp.pad(
        weight.reshape(rows, -1, NOPE + ROPE), ((0, 0), (0, 0), (0, LANES - NOPE - ROPE))
    ).reshape(rows, -1)


def from_slots(weight):
    rows = weight.shape[0]
    return weight.reshape(rows, -1, LANES)[:, :, : NOPE + ROPE].reshape(rows, -1)


def pack_rows(block, wide):
    rows, columns = block.shape
    parts = block.reshape(rows // 16, 16, columns)
    parts = jnp.pad(parts, ((0, 0), (0, 0), (0, wide - columns)))
    return parts.transpose(1, 0, 2).reshape(16, -1)


def unpack_rows(packed, wide, columns):
    count = packed.shape[2] // wide
    parts = packed.reshape(packed.shape[0], 16, count, wide)[..., :columns]
    return parts.transpose(0, 2, 1, 3).reshape(packed.shape[0], -1, columns)


def shards(
    block_input,
    out_grad,
    norm_gains,
    latent_weight,
    query_weight,
    keys_weight,
    output_weight,
    gate_weight,
    up_weight,
    down_weight,
    gains_moment,
    gains_second,
    latent_moment,
    latent_second,
    query_moment,
    query_second,
    keys_moment,
    keys_second,
    output_moment,
    output_second,
    gate_moment,
    gate_second,
    up_moment,
    up_second,
    down_moment,
    down_second,
):
    place = {name: lax.axis_index(name) for name in AXES}
    place["y"] = place["yh"] * 2 + place["yl"]
    group_index = place["c"] * RING + place["z"]
    tok_rows = block_input.shape[0]
    seq_rows = tok_rows * 2 * RING
    heads_here = output_weight.shape[0] // VDIM
    width = QR + KVR + ROPE
    gain_width = norm_gains.shape[0]

    latent_rows = latent_weight.shape[0]
    latent_pad = 24 - latent_rows
    gain_row = jnp.pad(to_low(norm_gains)[None], ((0, latent_pad - 1), (0, width - gain_width)))
    latent_block = jnp.concatenate([to_low(latent_weight), gain_row], axis=0)
    latent_mine = lax.all_to_all(
        jnp.broadcast_to(latent_block[None], (64,) + latent_block.shape),
        PLANE + ("z",),
        split_axis=0,
        concat_axis=0,
        tiled=True,
    )
    wide = heads_here * LANES
    key_cols = keys_weight.shape[1]
    small = swap(
        jnp.concatenate(
            [
                pack_rows(to_slots(to_low(query_weight)), wide),
                to_low(keys_weight),
                pack_rows(to_low(output_weight).T, 384),
            ],
            axis=1,
        )
    )
    tokens = swap(block_input).astype(jnp.float32)
    hidden_here = gate_weight.shape[1]
    fill = -hidden_here % LANES
    both = mix(
        *[jnp.pad(to_low(weight), ((0, 0), (0, fill))) for weight in (gate_weight, up_weight)]
    )
    cut = both.shape[1] - CELL
    weights_one = both[:, :cut]
    weights_two = jnp.pad(to_low(down_weight).T, ((0, 0), (0, fill)))
    weights_two = jnp.concatenate([both[:, cut:], weights_two], axis=1)
    weights_one = trade(weights_one, True)
    weights_two = trade(weights_two, False)
    cotangent = swap(out_grad)
    own_pos = (group_index * tok_rows + jnp.arange(tok_rows)).astype(jnp.float32)
    own_cos, own_sin = tables(own_pos)
    factor_one = lax.rsqrt(jnp.mean(tokens * tokens, axis=-1, keepdims=True) + EPS)
    spaced = tokens * factor_one
    spaced = jnp.pad(
        spaced.reshape(tok_rows, 8, 2, 8, latent_rows),
        ((0, 0), (0, 0), (0, 0), (0, 0), (0, latent_pad)),
    )
    core_first = place["c"] == 0
    spaced_mine = jnp.where(core_first, spaced[:, :, 0], spaced[:, :, 1]).reshape(tok_rows, -1)
    spaced_other = jnp.where(core_first, spaced[:, :, 1], spaced[:, :, 0]).reshape(tok_rows, -1)
    small = jnp.broadcast_to(small[None], (16,) + small.shape)
    latent_mine, spaced_mine, spaced_other, small = tie(
        [latent_mine, spaced_mine, spaced_other, small], weights_one, weights_two, cotangent
    )
    latent_other = send_core(latent_mine)
    small = exchange_plane(small)

    def in_cores(mine, other, extra):
        first = jnp.where(core_first, mine, other).reshape((8, 8) + extra)
        second = jnp.where(core_first, other, mine).reshape((8, 8) + extra)
        return jnp.stack([first, second], axis=1)

    gains_all = in_cores(
        latent_mine[:, latent_rows, :gain_width],
        latent_other[:, latent_rows, :gain_width],
        (gain_width,),
    )
    gains_all = gains_all.astype(jnp.float32).reshape(-1)
    gain_one = gains_all[:D]
    gain_two = gains_all[D : 2 * D]
    gain_query = gains_all[2 * D : 2 * D + QR]
    gain_keys = gains_all[2 * D + QR :]
    latent_full = in_cores(
        latent_mine[:, :latent_rows], latent_other[:, :latent_rows], (latent_rows, width)
    ).reshape(-1, width)

    normed = to_low(tokens * factor_one * gain_one)
    spaced_gain = jnp.pad(
        gain_one.reshape(8, 2, 8, latent_rows), ((0, 0), (0, 0), (0, 0), (0, latent_pad))
    )
    gain_mine = jnp.where(core_first, spaced_gain[:, 0], spaced_gain[:, 1]).reshape(-1)
    gain_other = jnp.where(core_first, spaced_gain[:, 1], spaced_gain[:, 0]).reshape(-1)
    latent = jnp.dot(
        to_low(spaced_mine * gain_mine),
        latent_mine.reshape(-1, width),
        preferred_element_type=jnp.float32,
    ) + jnp.dot(
        to_low(spaced_other * gain_other),
        latent_other.reshape(-1, width),
        preferred_element_type=jnp.float32,
    )
    query_part = latent[:, :QR]
    keys_part = latent[:, QR : QR + KVR]
    query_pre, factor_query = rms_forward(query_part, gain_query)
    keys_pre, factor_keys = rms_forward(keys_part, gain_keys)
    packed = jnp.concatenate(
        [
            to_low(query_pre),
            to_low(keys_pre),
            to_low(rotate(latent[:, QR + KVR :], own_cos, own_sin)),
        ],
        axis=1,
    )
    packed_pairs = gather_group(packed)
    cotangent = cotangent.astype(jnp.float32)
    gathered = to_abs([p[0] for p in packed_pairs], [p[1] for p in packed_pairs], place)
    cot_block = to_low(RESIDUAL * cotangent)
    gathered, cot_block, small, weights_one, weights_two = tie(
        [gathered, cot_block, small, weights_one, weights_two]
    )
    line_one = by_four(four_copies(weights_one), "x")
    line_two = first_y(weights_two, place)
    cot_all = joined(gather_group(cot_block))
    query_full = unpack_rows(small[:, :, : 3 * wide], wide, wide).reshape(-1, wide)
    keys_matrix = small[:, :, 3 * wide : 3 * wide + key_cols].reshape(-1, key_cols)
    output_turned = unpack_rows(small[:, :, 3 * wide + key_cols :], 384, SLICE).reshape(-1, SLICE)
    query_lat = gathered[:, :QR]
    keys_lat = gathered[:, QR : QR + KVR]
    shared_rot = gathered[:, QR + KVR :]
    factors = rope_slots(seq_rows)
    shared_slot = jnp.pad(shared_rot, ((0, 0), (NOPE, LANES - NOPE - ROPE)))
    queries, keys_all, keys_values, attended = attention(
        query_lat, keys_lat, query_full, keys_matrix, factors, shared_slot
    )
    attended, line_one, line_two, cot_all = tie([attended, line_one, line_two, cot_all])
    weights_one = by_four(four_copies(line_one), ("yl", "yh")).reshape(D, -1)
    weights_two = second_x(line_two, place).reshape(D, -1)
    down_turned = weights_two[:, CELL:]
    attended_mine, attended_other = to_rel(attended, place)

    def to_model(rows):
        return to_low(
            jnp.einsum("sa,da->sd", rows, output_turned, preferred_element_type=jnp.float32)
        )

    branch = scatter_halves(to_model(attended_mine), to_model(attended_other))
    hidden_state = tokens + RESIDUAL * branch
    mlp_pre, factor_two = rms_forward(hidden_state, gain_two)

    mlp_pairs = gather_group(to_low(mlp_pre))
    grad_hidden = jnp.dot(cot_all, down_turned, preferred_element_type=jnp.float32)
    grad_hidden, latent_full = tie([grad_hidden, latent_full])
    held, back_pairs = (), []
    for spot in (0, 1):
        near, far = mlp_pairs[2 * spot : 2 * spot + 2]
        *backs, rows, hidden, both = feed_forward(
            near + far, grad_hidden, weights_one, weights_two, held, spot
        )
        held = (rows, hidden, both)
        back_pairs += [backs[:2], backs[2:]]
    mlp_all, hidden_all, grad_both = held
    grad_mlp_in = scatter_group(back_pairs)
    grad_one = to_low(
        jnp.einsum("sd,sf->df", mlp_all, grad_both[:, :cut], preferred_element_type=jnp.float32)
    )
    grad_two = jnp.concatenate(
        [
            to_low(jnp.einsum("sd,sf->df", rows, part, preferred_element_type=jnp.float32))
            for rows, part in ((mlp_all, grad_both[:, cut:]), (cot_all, hidden_all))
        ],
        axis=1,
    )
    terms_one = by_four(grad_one.reshape(RING, -1, cut), ("yl", "yh"))
    grad_mlp_in, grad_two = tie([grad_mlp_in, grad_two], grad_one)
    fold_two = fold_x(grad_two.reshape(RING, -1, grad_two.shape[1]), place)

    grad_norm_two, grad_gain_two = rms_backward(grad_mlp_in, hidden_state, factor_two, gain_two)
    grad_state = cotangent + grad_norm_two
    branch_all = joined(gather_group(to_low(RESIDUAL * grad_state)))
    mlp_terms = [
        to_low(
            jnp.einsum(
                "sf,df->sd",
                hidden_all.reshape(RING, 2, tok_rows, -1)[:, index].reshape(RING * tok_rows, -1),
                down_turned,
                preferred_element_type=jnp.float32,
            )
        )
        for index in (0, 1)
    ]
    branch_all, *mlp_terms = tie([branch_all] + mlp_terms)
    attended_pairs = jnp.stack(
        [attended_mine.reshape(RING, tok_rows, -1), attended_other.reshape(RING, tok_rows, -1)],
        axis=1,
    ).reshape(seq_rows, -1)
    grad_output = to_low(
        jnp.einsum("sd,sa->da", branch_all, attended_pairs, preferred_element_type=jnp.float32)
    )
    grad_parts = to_low(
        jnp.dot(branch_all, output_turned, preferred_element_type=jnp.float32)
    ).reshape(RING, 2, tok_rows, -1)
    grad_attended = to_abs(
        [grad_parts[step, 0] for step in range(RING)],
        [grad_parts[step, 1] for step in range(RING)],
        place,
    )
    block_output = hidden_state + RESIDUAL * scatter_halves(*mlp_terms)
    grad_attended, normed = tie([grad_attended, normed])
    normed_cols = normed.reshape(tok_rows, 2 * RING, SLICE).transpose(1, 0, 2)
    normed_parts = []
    for step in range(RING):
        spot = (place["z"] + step) % RING
        pair = jnp.stack(
            [
                lax.dynamic_index_in_dim(normed_cols, core * RING + spot, axis=0, keepdims=False)
                for core in (place["c"], 1 - place["c"])
            ]
        )
        normed_parts.append(send_z(pair, step) if step else pair)
    normed_parts = jnp.stack(normed_parts)
    normed_all = jnp.stack([normed_parts[:, 0], send_core(normed_parts[:, 1])], axis=1)
    normed_all = normed_all.reshape(seq_rows, SLICE)
    grad_query_raw, grad_keys_raw, grad_shared = attention_back(
        queries, keys_all, keys_values, grad_attended, factors
    )
    grad_shared = grad_shared[:, NOPE : NOPE + ROPE]
    grad_query_w = to_low(
        jnp.einsum("sr,sc->rc", query_lat, grad_query_raw, preferred_element_type=jnp.float32)
    )
    grad_keys_w = to_low(
        jnp.einsum("sr,sc->rc", keys_lat, grad_keys_raw, preferred_element_type=jnp.float32)
    )
    small_grads = jnp.concatenate(
        [
            jax.vmap(lambda block: pack_rows(block, wide))(grad_query_w.reshape(16, -1, wide)),
            grad_keys_w.reshape(16, 16, key_cols),
            jax.vmap(lambda block: pack_rows(block, 384))(grad_output.reshape(16, -1, SLICE)),
        ],
        axis=2,
    )
    latent_terms = to_low(
        jnp.concatenate(
            [
                jnp.einsum(
                    "sc,rc->sr", grad_query_raw, query_full, preferred_element_type=jnp.float32
                ),
                jnp.einsum(
                    "sc,rc->sr", grad_keys_raw, keys_matrix, preferred_element_type=jnp.float32
                ),
                grad_shared,
            ],
            axis=1,
        )
    )
    latent_terms, block_output, small_grads, terms_one, fold_two = tie(
        [latent_terms, block_output, small_grads, terms_one, fold_two]
    )
    block_output = swap(block_output)
    terms_one = by_four(add_up(terms_one).reshape(RING, -1, cut), "x")
    sum_two = trade_back(fold_y(fold_two.reshape(RING, -1, fold_two.shape[1]), place), False)
    sum_down = sum_two[:, CELL : CELL + hidden_here].astype(jnp.float32).T
    grad_latent_in = scatter_halves(*to_rel(latent_terms, place))
    grad_latent_in, small_grads, terms_one = tie([grad_latent_in, small_grads, terms_one])
    sum_one = trade_back(add_up(terms_one), True)
    sum_gate, sum_up = (
        part[:, :hidden_here].astype(jnp.float32)
        for part in unmix(jnp.concatenate([sum_one, sum_two[:, :CELL]], axis=1))
    )
    small_terms = exchange_plane(small_grads)
    grad_query_pre, grad_gain_query = rms_backward(
        grad_latent_in[:, :QR], query_part, factor_query, gain_query
    )
    grad_keys_pre, grad_gain_keys = rms_backward(
        grad_latent_in[:, QR : QR + KVR], keys_part, factor_keys, gain_keys
    )
    grad_rope = unrotate(grad_latent_in[:, QR + KVR :], own_cos, own_sin)
    grad_latent = to_low(jnp.concatenate([grad_query_pre, grad_keys_pre, grad_rope], axis=1))
    grad_normed = jnp.einsum(
        "sc,dc->sd", grad_latent, latent_full, preferred_element_type=jnp.float32
    )
    grad_norm_one, grad_gain_one = rms_backward(grad_normed, tokens, factor_one, gain_one)
    input_grad = swap(grad_state + grad_norm_one)

    latent_grads = joined(gather_group(grad_latent))
    grad_latent_w = jnp.einsum(
        "sd,sc->dc",
        normed_all,
        latent_grads,
        preferred_element_type=jnp.float32,
    )
    grad_gains = jnp.concatenate(
        [grad_gain_one, grad_gain_two, grad_gain_query, grad_gain_keys]
    ).reshape(2, RING, -1)
    gains_line = lax.dynamic_index_in_dim(grad_gains, place["c"], axis=0, keepdims=False)
    gains_line = gains_line + send_core(
        lax.dynamic_index_in_dim(grad_gains, 1 - place["c"], axis=0, keepdims=False)
    )


    def gains_at(step):
        spot = (place["z"] + step) % RING
        return lax.dynamic_index_in_dim(gains_line, spot, axis=0, keepdims=True)

    gains_sum = gains_at(0)
    for step in (1, 2, 3):
        gains_sum = gains_sum + send_z(gains_at(step), step)
    gains_rows = jnp.pad(gains_sum.reshape(16, 1, gain_width), ((0, 0), (0, 0), (0, width - gain_width)))
    last = to_low(jnp.concatenate([grad_latent_w.reshape(16, -1, width), gains_rows], axis=1))
    last, small_terms = tie([last, small_terms])
    sum_small = swap(add_up(small_terms)).astype(jnp.float32)
    sum_query = from_slots(unpack_rows(sum_small[None, :, : 3 * wide], wide, wide)[0])
    sum_keys = sum_small[:, 3 * wide : 3 * wide + key_cols]
    sum_output = unpack_rows(sum_small[None, :, 3 * wide + key_cols :], 384, SLICE)[0].T
    last = scatter_plane(last)
    route = []
    for source in range(128):
        rest, at_z = divmod(source, 4)
        rest, at_yh = divmod(rest, 2)
        rest, at_c = divmod(rest, 2)
        at_yl, at_x = divmod(rest, 4)
        route.append((source, 16 * (at_c * 4 + at_z) + (at_yl * 4 + at_x) * 2 + at_yh))
    last = lax.ppermute(last, AXES, route).astype(jnp.float32)
    sum_latent = last[:-1]
    sum_gains = last[-1, :gain_width]

    rates = rate_table()
    next_gains, moment_gains, second_gains = adamw(
        norm_gains, sum_gains, gains_moment, gains_second, rates[0], 0.0
    )
    next_latent, moment_latent, second_latent = adamw(
        latent_weight, sum_latent, latent_moment, latent_second, rates[1], 0.1
    )
    next_query, moment_query, second_query = adamw(
        query_weight, sum_query, query_moment, query_second, rates[2], 0.1
    )
    next_keys, moment_keys, second_keys = adamw(
        keys_weight, sum_keys, keys_moment, keys_second, rates[3], 0.1
    )
    next_output, moment_output, second_output = adamw(
        output_weight, sum_output, output_moment, output_second, rates[4], 0.1
    )
    next_gate, moment_gate, second_gate = adamw(
        gate_weight, sum_gate, gate_moment, gate_second, rates[5], 0.1
    )
    next_up, moment_up, second_up = adamw(
        up_weight, sum_up, up_moment, up_second, rates[6], 0.1
    )
    next_down, moment_down, second_down = adamw(
        down_weight, sum_down, down_moment, down_second, rates[7], 0.1
    )
    return (
        block_output,
        input_grad,
        next_gains,
        moment_gains,
        second_gains,
        next_latent,
        moment_latent,
        second_latent,
        next_query,
        moment_query,
        second_query,
        next_keys,
        moment_keys,
        second_keys,
        next_output,
        moment_output,
        second_output,
        next_gate,
        moment_gate,
        second_gate,
        next_up,
        moment_up,
        second_up,
        next_down,
        moment_down,
        second_down,
    )


def solution(mesh):
    devices = jax.sharding.Mesh(mesh.devices.reshape(SIZES), AXES)
    rows, split = ("yl", "x", "c"), ("yh", "z")
    whole = rows + split
    tokens, flat = P(whole, None), P(whole)
    by_rows, by_cols = P(rows, split), P(split, rows)
    weights = (flat, tokens, by_rows, by_rows, by_cols, by_rows, by_rows, by_cols)
    return jax.shard_map(
        shards,
        mesh=devices,
        in_specs=(tokens, tokens) + weights + tuple(s for s in weights for _ in range(2)),
        out_specs=(tokens, tokens) + tuple(s for s in weights for _ in range(3)),
        check_vma=False,
    )
```

time: 1800 us -> 856 us (0.48)
  waiting for transfers between devices: 1370 us -> 233 us
  starting transfers between devices: 1.64 us -> 193 us
  blocking collectives: 175 us -> 0 us
  local copies, waits for them, and re-layouts: 25 us -> 152 us
  matrix products: 158 us -> 82.6 us
  other arithmetic: 46.2 us -> 117 us
  Pallas kernels: 0 us -> 60.5 us
    all_gather x9 -> x0, waiting for transfers between devices: 618 us -> none  [the longest x1 246 us: shards(): lax.all_gather(to_low(latent_weight), ('dp', 'tensor'), axis=0, tiled=True)]
    reduce_scatter x9 -> x0, waiting for transfers between devices: 566 us -> none  [the longest x1 89.3 us: shards(): lax.psum_scatter(jnp.dot(attended, output_full, preferred_element_type=jn...]
    unnamed x22 -> x0, waiting for transfers between devices: 185 us -> none
    ppermute x0 -> x98, waiting for transfers between devices: none -> 180 us  [the longest x42 55 us: send_z(): return lax.ppermute(block, 'z', ring(step))]
    ppermute x0 -> x98, starting transfers between devices: none -> 139 us  [the longest x42 47.1 us: send_z(): return lax.ppermute(block, 'z', ring(step))]
    unnamed x2 -> x0, blocking collectives: 139 us -> none
    dot_general x28 -> x13, matrix products: 145 us -> 71.5 us  [the longest x2 15.1 us: shards(): jnp.einsum('sd,sf->df', rows, part, preferred_element_type=jnp.float32)]
    pallas_call x0 -> x15, Pallas kernels: none -> 60.5 us  [the longest x2 34 us: feed_forward(): pl.pallas_call(ff_kernel, grid=(steps,), in_specs=[whole] * 4 + [pl.Block...]
  transfers between devices with their start and end apart: 20 -> 106, of which waited for: 20 -> 32; matrix products, arithmetic and copies ran while one was open for 7% -> 33% of each run, Pallas kernels for 0% -> 5%
where the time goes in v1:
time: 856 us; the launch traced here: 842 us
  waiting for transfers between devices  233 us (27%)
  starting transfers between devices  193 us (23%)
  local copies, waits for them, and re-layouts  152 us (18%)
  other arithmetic  117 us (14%)
  matrix products  82.6 us (10%)
  Pallas kernels  60.5 us (7%)
    ppermute x42, waiting for transfers between devices, send_z(): return lax.ppermute(block, 'z', ring(step))  55 us
    unnamed x270, local copies, waits for them, and re-layouts  48.8 us
    ppermute x42, starting transfers between devices, send_z(): return lax.ppermute(block, 'z', ring(step))  47.1 us
    ppermute x6, waiting for transfers between devices, swap(): return lax.ppermute(block, ('c', 'yh'), [(0, 0), (1, 2), (2, 1), (3, 3)])  43 us
    all_to_all x3, waiting for transfers between devices, exchange_plane(): lax.all_to_all(blocks, PLANE, split_axis=0, concat_axis=0, tiled=True)  42 us
    ppermute x2, waiting for transfers between devices, trade_back(): return lax.ppermute(block, ('yl', 'x', 'c', 'yh'), back)  38.7 us
    pallas_call x2, Pallas kernels, feed_forward(): pl.pallas_call(ff_kernel, grid=(steps,), in_specs=[whole] * 4 + [pl.Block...  34 us
    ppermute x30, starting transfers between devices, send_core(): return lax.ppermute(block, 'c', [(0, 1), (1, 0)])  32.6 us
  transfers between devices with their start and end apart: 106, of which 32 were waited for; matrix products, arithmetic and copies ran while one was open for 33% of the time, Pallas kernels for 5%

profile of v1, /device:TPU:5, one launch (start us, length us, event | category | flops | bytes accessed | tf_op | source)
XLA Modules:
  0.0 841.9 jit_solution(13944962780276762584)
XLA Ops:
  12.0 9.2 %all-to-all-start = ((bf16[64,24,1056]{2,1,0:T(8,128)(2,1)}), bf16[64,24,1056]{2,1,0:T(8,128)(2,1)}, u32[]{:S(2)}, u32[]{:S(2)}) async-start(bf16[64,24,1056]{2,1,0:T(8,128)(2,1)} %broadcast_in_dim.25), calls=%async_computation | async-start | bytes 7077888 | tf_op jit(solution)/shard_map/all_to_all | solution.py:654
  40.7 43.0 %collective-permute-done = bf16[128,2560]{1,0:T(8,128)(2,1)S(1)} collective-permute-done((bf16[128,2560]{1,0:T(8,128)(2,1)}, bf16[128,2560]{1,0:T(8,128)(2,1)S(1)}, u32[]{:S(2)}, u32[]{:S(2)}) %collective-permute-start) | collective-permute-done | bytes 655392 | tf_op jit(solution)/shard_map/ppermute | solution.py:123
  115.7 7.9 all-to-all-start.1
  142.9 30.3 %all-to-all-done.1.refs_2_ = bf16[16,16,6400]{2,1,0:T(8,128)(2,1)} async-done(((bf16[16,16,6400]{2,1,0:T(8,128)(2,1)}), bf16[16,16,6400]{2,1,0:T(8,128)(2,1)}, u32[]{:S(2)}, u32[]{:S(2)}) %all-to-all-start.1) | async-done | bytes 3276832 | tf_op jit(solution)/shard_map/all_to_all | solution.py:426
  196.7 10.5 %attention.1 = (bf16[1024,640]{1,0:T(8,128)(2,1)S(1)}, bf16[1024,640]{1,0:T(8,128)(2,1)}, bf16[1024,640]{1,0:T(8,128)(2,1)}, bf16[1024,320]{1,0:T(8,128)(2,1)S(1)}) custom-call(bf16[1024,768]{1,0:T(8,128)(2,1)} %slice.497.query_ref, bf16[1024,256]{1,0:T(8,128)(2,1)S(1)} %slice.498.keys_ref, bf16[768,640]{1,0:T(8,128)(2,1)S(1)} %bitcast.232, ...), custom_call_target="tpu_custom_call" | custom-call | flops 2684354560 | bytes 8388608 | tf_op jit(solution)/shard_map/attention/pallas_call | solution.py:498
  261.9 10.2 %reshape.380.refs_1_ = bf16[2560,1056]{1,0:T(8,128)(2,1)} reshape(bf16[8,2,8,20,1056]{4,3,2,1,0:T(8,128)(2,1)} %pad_maximum_fusion) | data formatting | bytes 10813440 | tf_op jit(solution)/shard_map/reshape | solution.py:721
  285.3 5.7 all-to-all-start.3
  333.5 7.9 collective-permute-done.31.refs_2_
  341.5 8.7 %fusion.2.refs_0_ = f32[1024,896]{1,0:T(8,128)} fusion(bf16[1024,2560]{1,0:T(8,128)(2,1)} %get-tuple-element.93, bf16[2560,1152]{1,0:T(8,128)(2,1)S(1)} %bitcast.251), kind=kOutput, calls=%fused_computation.16 | convolution fusion | flops 4697620480 | bytes 13500416 | tf_op jit(solution)/shard_map/dot_general | solution.py:787
  358.4 5.9 collective-permute-done.41
  368.0 11.1 %all-to-all-done.3 = bf16[4,4,160,1536]{3,2,1,0:T(8,128)(2,1)} async-done(((bf16[4,4,160,1536]{3,2,1,0:T(8,128)(2,1)}), bf16[4,4,160,1536]{3,2,1,0:T(8,128)(2,1)}, u32[]{:S(2)}, u32[]{:S(2)}) %all-to-all-start.3) | async-done | bytes 7864352 | tf_op jit(solution)/shard_map/all_to_all | solution.py:309
  381.3 16.5 %feed_forward.2 = (bf16[128,2560]{1,0:T(8,128)(2,1)S(1)}, bf16[128,2560]{1,0:T(8,128)(2,1)}, bf16[128,2560]{1,0:T(8,128)(2,1)S(1)}, bf16[128,2560]{1,0:T(8,128)(...) custom-call(bf16[128,2560]{1,0:T(8,128)(2,1)S(1)} %multiply_convert_fusion.2.refs_0_, ...), custom_call_target="tpu_custom_call" | custom-call | flops 9395240960 | bytes 20971520 | tf_op jit(solution)/shard_map/feed_forward/pallas_call | solution.py:369
  398.6 17.5 %feed_forward.3 = (bf16[128,2560]{1,0:T(8,128)(2,1)S(1)}, bf16[128,2560]{1,0:T(8,128)(2,1)}, bf16[128,2560]{1,0:T(8,128)(2,1)S(1)}, bf16[128,2560]{1,0:T(8,128)(...) custom-call(bf16[128,2560]{1,0:T(8,128)(2,1)} %constant_dynamic-upda, ...), custom_call_target="tpu_custom_call", output_to_operand_aliasing={{4}: (7, {}), {5}: (8, {}), {6}: (9, {})} | custom-call | flops 9395240960 | bytes 20971520 | tf_op jit(solution)/shard_map/feed_forward/pallas_call | solution.py:369
  421.6 10.8 %convolution_convert_fusion.refs_2_ = bf16[2560,1536]{1,0:T(8,128)(2,1)} fusion(bf16[1024,2560]{1,0:T(8,128)(2,1)S(1)} %copy-done.113, bf16[1024,1792]{1,0:T(8,128)(2,1)S(1)} %copy-done.114), kind=kOutput, calls=%fused_computation | convolution fusion | flops 8056995840 | bytes 16252928 | tf_op jit(solution)/shard_map/sd,sf->df/dot_general | solution.py:800
  432.4 9.7 %convolution_convert_fusion.1 = bf16[2560,896]{1,0:T(8,128)(2,1)} fusion(bf16[1024,2560]{1,0:T(8,128)(2,1)} %get-tuple-element.93, bf16[1024,896]{1,0:T(8,128)(2,1)S(1)} %copy-done.58), kind=kOutput, calls=%fused_computation.3 | convolution fusion | flops 4699914240 | bytes 11665408 | tf_op jit(solution)/shard_map/sd,sf->df/dot_general | solution.py:804
  443.6 5.6 all-to-all-start.4
  449.2 5.7 pad_maximum_fusion.1.refs_1_
  460.6 6.1 collective-permute-done.45
  474.1 7.8 collective-permute-done.46
  499.2 6.6 convolution_convert_fusion.2.refs_2_
  537.7 16.0 %attention_back.1 = (bf16[1024,640]{1,0:T(8,128)(2,1)S(1)}, bf16[1024,640]{1,0:T(8,128)(2,1)S(1)}, f32[1024,128]{1,0:T(8,128)S(1)}) custom-call(bf16[1024,640]{1,0:T(8,128)(2,1)} %copy-done.19, bf16[1024,640]{1,0:T(8,128)(2,1)} %get-tuple-element.86.k_ref, bf16[1024,640]{1,0:T(8,128)(2,1)} %get-tuple-element.87.kv_ref, bf16[1024,320]{1,0:T(8,128)(2,1)S(1)} %copy-done.1, ...), custom_call_target="tpu_custom_call" | custom-call | flops 6710886400 | bytes 10485760 | tf_op jit(solution)/shard_map/attention_back/pallas_call | solution.py:574
  566.4 5.7 convolution_convert_fusion.6
  605.7 19.6 %collective-permute-done.66 = bf16[640,1152]{1,0:T(8,128)(2,1)S(1)} collective-permute-done((bf16[640,1152]{1,0:T(8,128)(2,1)S(1)}, bf16[640,1152]{1,0:T(8,128)(2,1)S(1)}, u32[]{:S(2)}, u32[]{:S(2)}) %collective-permute-start.66) | collective-permute-done | bytes 1474592 | tf_op jit(solution)/shard_map/ppermute | solution.py:110
  648.1 6.3 reduce_sum.161
  654.4 7.2 all-to-all-start.5
  664.6 9.3 %collective-permute-start.96 = (bf16[160,1152]{1,0:T(8,128)(2,1)}, bf16[160,1152]{1,0:T(8,128)(2,1)}, u32[]{:S(2)}, u32[]{:S(2)}) collective-permute-start(bf16[160,1152]{1,0:T(8,128)(2,1)} %pad_maximum_fusion.28), channel_id=1, source_target_pairs={{0,68},{64,0},{4,64},{68,4},{1,69},{65,1},{5,65},{69,5},{2,70},{66... | collective-permute-start | bytes 1105928 | tf_op jit(solution)/shard_map/ppermute | solution.py:115
  692.8 8.8 %collective-permute-done.97 = bf16[160,1152]{1,0:T(8,128)(2,1)S(1)} collective-permute-done((bf16[160,1152]{1,0:T(8,128)(2,1)S(1)}, bf16[160,1152]{1,0:T(8,128)(2,1)S(1)}, u32[]{:S(2)}, u32[]{:S(2)}) %collective-permute-start.97) | collective-permute-done | bytes 368672 | tf_op jit(solution)/shard_map/ppermute | solution.py:305
  721.0 5.9 fusion.16
  758.3 29.9 %collective-permute-done.92 = bf16[160,1536]{1,0:T(8,128)(2,1)S(1)} collective-permute-done((bf16[160,1536]{1,0:T(8,128)(2,1)}, bf16[160,1536]{1,0:T(8,128)(2,1)S(1)}, u32[]{:S(2)}, u32[]{:S(2)}) %collective-permute-start.92) | collective-permute-done | bytes 491552 | tf_op jit(solution)/shard_map/ppermute | solution.py:305
  801.6 7.9 all-to-all-start.7
  814.2 11.7 %all-to-all-done.7 = bf16[16,21,1056]{2,1,0:T(8,128)(2,1)S(1)} async-done(((bf16[16,21,1056]{2,1,0:T(8,128)(2,1)}), bf16[16,21,1056]{2,1,0:T(8,128)(2,1)S(1)}, u32[]{:S(2)}, u32[]{:S(2)}) %all-to-all-start.7) | async-done | bytes 709664 | tf_op jit(solution)/shard_map/all_to_all | solution.py:426
  831.2 5.6 collective-permute-done.90
  (717 shorter events, 467.3 us)
Async XLA Ops:
  4.5 88.3 %collective-permute-start.1 = (bf16[16,6400]{1,0:T(8,128)(2,1)}, bf16[16,6400]{1,0:T(8,128)(2,1)}, u32[]{:S(2)}, u32[]{:S(2)}) collective-permute-start(bf16[16,6400]{1,0:T(8,128)(2,1)} %pad_maximum_fusion.38), channel_id=1, source_target_pairs={{0,0},{4,8},{8,4},{12,12},{1,1},{5,9},{9,5},{13,13},{2,2},{6,10},{... | collective-permute-start | bytes 614408 | tf_op jit(solution)/shard_map/ppermute | solution.py:123
  12.0 80.8 %all-to-all-start = ((bf16[64,24,1056]{2,1,0:T(8,128)(2,1)}), bf16[64,24,1056]{2,1,0:T(8,128)(2,1)}, u32[]{:S(2)}, u32[]{:S(2)}) async-start(bf16[64,24,1056]{2,1,0:T(8,128)(2,1)} %broadcast_in_dim.25), calls=%async_computation | async-start | bytes 7077888 | tf_op jit(solution)/shard_map/all_to_all | solution.py:654
  23.1 69.6 %collective-permute-start.3 = (bf16[160,1152]{1,0:T(8,128)(2,1)}, bf16[160,1152]{1,0:T(8,128)(2,1)}, u32[]{:S(2)}, u32[]{:S(2)}) collective-permute-start(bf16[160,1152]{1,0:T(8,128)(2,1)} %fusion.47), channel_id=1, source_target_pairs={{0,0},{4,8},{8,4},{12,12},{16,64},{20,72},{24,68},{28,76},{32,16},... | collective-permute-start | bytes 1105928 | tf_op jit(solution)/shard_map/ppermute | solution.py:300
  27.8 55.8 %collective-permute-start = (bf16[128,2560]{1,0:T(8,128)(2,1)}, bf16[128,2560]{1,0:T(8,128)(2,1)S(1)}, u32[]{:S(2)}, u32[]{:S(2)}) collective-permute-start(bf16[128,2560]{1,0:T(8,128)(2,1)} %param.26), channel_id=1, source_target_pairs={{0,0},{4,8},{8,4},{12,12},{1,1},{5,9},{9,5},{13,13},{2,2},{6,10},{... | collective-permute-start | bytes 1966088 | tf_op jit(solution)/shard_map/ppermute | solution.py:123
  34.0 58.7 %collective-permute-start.2 = (bf16[160,1536]{1,0:T(8,128)(2,1)}, bf16[160,1536]{1,0:T(8,128)(2,1)S(1)}, u32[]{:S(2)}, u32[]{:S(2)}) collective-permute-start(bf16[160,1536]{1,0:T(8,128)(2,1)} %slice_dynamic-update-slice_fusion), channel_id=1, source_target_pairs={{0,0},{4,8},{8,16},{12,24},{16,32},{20,40},{24,48},{28,56},{32,4},... | collective-permute-start | bytes 1474568 | tf_op jit(solution)/shard_map/ppermute | solution.py:300
  38.6 54.2 %collective-permute-start.4 = (bf16[128,2560]{1,0:T(8,128)(2,1)}, bf16[128,2560]{1,0:T(8,128)(2,1)S(1)}, u32[]{:S(2)}, u32[]{:S(2)}) collective-permute-start(bf16[128,2560]{1,0:T(8,128)(2,1)} %param.27), channel_id=1, source_target_pairs={{0,0},{4,8},{8,4},{12,12},{1,1},{5,9},{9,5},{13,13},{2,2},{6,10},{... | collective-permute-start | bytes 1966088 | tf_op jit(solution)/shard_map/ppermute | solution.py:123
  115.7 57.5 %all-to-all-start.1 = ((bf16[16,16,6400]{2,1,0:T(8,128)(2,1)}), bf16[16,16,6400]{2,1,0:T(8,128)(2,1)}, u32[]{:S(2)}, u32[]{:S(2)}) async-start(bf16[16,16,6400]{2,1,0:T(8,128)(2,1)} %get-tuple-element.82), calls=%async_computation.1 | async-start | bytes 6553600 | tf_op jit(solution)/shard_map/all_to_all | solution.py:426
  173.2 44.5 %collective-permute-start.16 = (bf16[160,1152]{1,0:T(8,128)(2,1)}, bf16[160,1152]{1,0:T(8,128)(2,1)}, u32[]{:S(2)}, u32[]{:S(2)}) collective-permute-start(bf16[160,1152]{1,0:T(8,128)(2,1)} %get-tuple-element.90), channel_id=1, source_target_pairs={{0,68},{64,0},{4,64},{68,4},{1,69},{65,1},{5,65},{69,5},{2,70},{66... | collective-permute-start | bytes 1105928 | tf_op jit(solution)/shard_map/ppermute | solution.py:115
  173.5 46.9 %collective-permute-start.15 = (bf16[160,1152]{1,0:T(8,128)(2,1)}, bf16[160,1152]{1,0:T(8,128)(2,1)}, u32[]{:S(2)}, u32[]{:S(2)}) collective-permute-start(bf16[160,1152]{1,0:T(8,128)(2,1)} %get-tuple-element.90), channel_id=1, source_target_pairs={{0,4},{64,68},{4,0},{68,64},{1,5},{65,69},{5,1},{69,65},{2,6},{66,... | collective-permute-start | bytes 1105928 | tf_op jit(solution)/shard_map/ppermute | solution.py:115
  175.1 45.3 %collective-permute-start.14 = (bf16[160,1152]{1,0:T(8,128)(2,1)}, bf16[160,1152]{1,0:T(8,128)(2,1)}, u32[]{:S(2)}, u32[]{:S(2)}) collective-permute-start(bf16[160,1152]{1,0:T(8,128)(2,1)} %get-tuple-element.90), channel_id=1, source_target_pairs={{0,64},{64,4},{4,68},{68,0},{1,65},{65,5},{5,69},{69,1},{2,66},{66... | collective-permute-start | bytes 1105928 | tf_op jit(solution)/shard_map/ppermute | solution.py:115
  177.2 46.1 %collective-permute-start.21 = (bf16[128,2560]{1,0:T(8,128)(2,1)}, bf16[128,2560]{1,0:T(8,128)(2,1)}, u32[]{:S(2)}, u32[]{:S(2)}) collective-permute-start(bf16[128,2560]{1,0:T(8,128)(2,1)} %get-tuple-element.91), channel_id=1, source_target_pairs={{0,3},{1,0},{2,1},{3,2},{4,7},{5,4},{6,5},{7,6},{8,11},{9,8},{10,9... | collective-permute-start | bytes 1966088 | tf_op jit(solution)/shard_map/ppermute | solution.py:106
  179.2 47.8 %collective-permute-start.18 = (bf16[128,2560]{1,0:T(8,128)(2,1)}, bf16[128,2560]{1,0:T(8,128)(2,1)}, u32[]{:S(2)}, u32[]{:S(2)}) collective-permute-start(bf16[128,2560]{1,0:T(8,128)(2,1)} %get-tuple-element.91), channel_id=1, source_target_pairs={{0,1},{1,2},{2,3},{3,0},{4,5},{5,6},{6,7},{7,4},{8,9},{9,10},{10,1... | collective-permute-start | bytes 1966088 | tf_op jit(solution)/shard_map/ppermute | solution.py:106
  210.6 35.1 %all-to-all-start.2 = ((bf16[4,160,1536]{2,1,0:T(8,128)(2,1)}), bf16[4,160,1536]{2,1,0:T(8,128)(2,1)S(1)}, u32[]{:S(2)}, u32[]{:S(2)}) async-start(bf16[4,160,1536]{2,1,0:T(8,128)(2,1)} %broadcast_in_dim.30), calls=%async_computation.2 | async-start | bytes 3932160 | tf_op jit(solution)/shard_map/all_to_all | solution.py:309
  253.7 37.2 %collective-permute-start.25 = (bf16[512,2560]{1,0:T(8,128)(2,1)}, bf16[512,2560]{1,0:T(8,128)(2,1)}, u32[]{:S(2)}, u32[]{:S(2)}) collective-permute-start(bf16[512,2560]{1,0:T(8,128)(2,1)} %convolution_convert_fusion.4), channel_id=1, source_target_pairs={{0,8},{8,0},{1,9},{9,1},{2,10},{10,2},{3,11},{11,3},{4,12},{12,4},... | collective-permute-start | bytes 7864328 | tf_op jit(solution)/shard_map/ppermute | solution.py:119
  272.1 40.2 %collective-permute-start.35 = (bf16[4,160,1152]{2,1,0:T(8,128)(2,1)}, bf16[4,160,1152]{2,1,0:T(8,128)(2,1)}, u32[]{:S(2)}, u32[]{:S(2)}) collective-permute-start(bf16[4,160,1152]{2,1,0:T(8,128)(2,1)} %get-tuple-element.94), channel_id=1, source_target_pairs={{0,48},{16,0},{32,16},{48,32},{1,49},{17,1},{33,17},{49,33},{2,50}... | collective-permute-start | bytes 4423688 | tf_op jit(solution)/shard_map/ppermute | solution.py:110
  272.6 41.5 %collective-permute-start.33 = (bf16[4,160,1152]{2,1,0:T(8,128)(2,1)}, bf16[4,160,1152]{2,1,0:T(8,128)(2,1)}, u32[]{:S(2)}, u32[]{:S(2)}) collective-permute-start(bf16[4,160,1152]{2,1,0:T(8,128)(2,1)} %get-tuple-element.94), channel_id=1, source_target_pairs={{0,16},{16,32},{32,48},{48,0},{1,17},{17,33},{33,49},{49,1},{2,18}... | collective-permute-start | bytes 4423688 | tf_op jit(solution)/shard_map/ppermute | solution.py:110
  285.3 93.8 %all-to-all-start.3 = ((bf16[4,4,160,1536]{3,2,1,0:T(8,128)(2,1)}), bf16[4,4,160,1536]{3,2,1,0:T(8,128)(2,1)}, u32[]{:S(2)}, u32[]{:S(2)}) async-start(bf16[4,4,160,1536]{3,2,1,0:T(8,128)(2,1)} %broadcast_in_dim.35), calls=%async_computation.3 | async-start | bytes 15728640 | tf_op jit(solution)/shard_map/all_to_all | solution.py:309
  357.2 41.4 %collective-permute-start.43 = (bf16[128,2560]{1,0:T(8,128)(2,1)}, bf16[128,2560]{1,0:T(8,128)(2,1)}, u32[]{:S(2)}, u32[]{:S(2)}) collective-permute-start(bf16[128,2560]{1,0:T(8,128)(2,1)} %collective-permute-done.40.refs_2_), channel_id=1, source_target_pairs={{0,8},{8,0},{1,9},{9,1},{2,10},{10,2},{3,11},{11,3},{4,12},{12,4},... | collective-permute-start | bytes 1966088 | tf_op jit(solution)/shard_map/ppermute | solution.py:119
  365.1 33.5 %collective-permute-start.42 = (bf16[128,2560]{1,0:T(8,128)(2,1)}, bf16[128,2560]{1,0:T(8,128)(2,1)}, u32[]{:S(2)}, u32[]{:S(2)}) collective-permute-start(bf16[128,2560]{1,0:T(8,128)(2,1)} %constant_dynamic-update-slice_fusion.11.refs_0_), channel_id=1, source_target_pairs={{0,8},{8,0},{1,9},{9,1},{2,10},{10,2},{3,11},{11,3},{4,12},{12,4},... | collective-permute-start | bytes 1966088 | tf_op jit(solution)/shard_map/ppermute | solution.py:119
  443.6 186.9 %all-to-all-start.4 = ((bf16[4,640,1536]{2,1,0:T(8,128)(2,1)}), bf16[4,640,1536]{2,1,0:T(8,128)(2,1)}, u32[]{:S(2)}, u32[]{:S(2)}) async-start(bf16[4,640,1536]{2,1,0:T(8,128)(2,1)} %bitcast.239), calls=%async_computation.4 | async-start | bytes 15728640 | tf_op jit(solution)/shard_map/all_to_all | solution.py:309
  603.1 38.7 %collective-permute-start.77 = (bf16[4,128,320]{1,2,0:T(8,128)(2,1)S(1)}, bf16[4,128,320]{1,2,0:T(8,128)(2,1)}, u32[]{:S(2)}, u32[]{:S(2)}) collective-permute-start(bf16[4,128,320]{1,2,0:T(8,128)(2,1)S(1)} %get-tuple-element.251), channel_id=1, source_target_pairs={{0,8},{8,0},{1,9},{9,1},{2,10},{10,2},{3,11},{11,3},{4,12},{12,4},... | collective-permute-start | bytes 983048 | tf_op jit(solution)/shard_map/ppermute | solution.py:119
  639.3 35.7 %collective-permute-start.68 = (bf16[512,1056]{0,1:T(8,128)(2,1)}, bf16[512,1056]{0,1:T(8,128)(2,1)}, u32[]{:S(2)}, u32[]{:S(2)}) collective-permute-start(bf16[512,1056]{0,1:T(8,128)(2,1)} %copy.212), channel_id=1, source_target_pairs={{0,8},{8,0},{1,9},{9,1},{2,10},{10,2},{3,11},{11,3},{4,12},{12,4},... | collective-permute-start | bytes 3244040 | tf_op jit(solution)/shard_map/ppermute | solution.py:119
  645.0 58.7 %collective-permute-start.67 = (f32[128,2560]{1,0:T(8,128)}, f32[128,2560]{1,0:T(8,128)}, u32[]{:S(2)}, u32[]{:S(2)}) collective-permute-start(f32[128,2560]{1,0:T(8,128)} %get-tuple-element.120), channel_id=1, source_target_pairs={{0,0},{4,8},{8,4},{12,12},{1,1},{5,9},{9,5},{13,13},{2,2},{6,10},{... | collective-permute-start | bytes 3932168 | tf_op jit(solution)/shard_map/ppermute | solution.py:123
  654.4 50.2 %all-to-all-start.5 = ((bf16[4,160,1536]{2,1,0:T(8,128)(2,1)}), bf16[4,160,1536]{2,1,0:T(8,128)(2,1)S(1)}, u32[]{:S(2)}, u32[]{:S(2)}) async-start(bf16[4,160,1536]{2,1,0:T(8,128)(2,1)} %bitcast.248), calls=%async_computation.5 | async-start | bytes 3932160 | tf_op jit(solution)/shard_map/all_to_all | solution.py:309
  713.4 36.7 %collective-permute-start.82 = (bf16[128,1056]{1,0:T(8,128)(2,1)}, bf16[128,1056]{1,0:T(8,128)(2,1)}, u32[]{:S(2)}, u32[]{:S(2)}) collective-permute-start(bf16[128,1056]{1,0:T(8,128)(2,1)} %concatenate.207), channel_id=1, source_target_pairs={{0,3},{1,0},{2,1},{3,2},{4,7},{5,4},{6,5},{7,6},{8,11},{9,8},{10,9... | collective-permute-start | bytes 811016 | tf_op jit(solution)/shard_map/ppermute | solution.py:106
  715.9 35.5 %collective-permute-start.79 = (bf16[128,1056]{1,0:T(8,128)(2,1)}, bf16[128,1056]{1,0:T(8,128)(2,1)}, u32[]{:S(2)}, u32[]{:S(2)}) collective-permute-start(bf16[128,1056]{1,0:T(8,128)(2,1)} %concatenate.207), channel_id=1, source_target_pairs={{0,1},{1,2},{2,3},{3,0},{4,5},{5,6},{6,7},{7,4},{8,9},{9,10},{10,1... | collective-permute-start | bytes 811016 | tf_op jit(solution)/shard_map/ppermute | solution.py:106
  715.9 37.7 %collective-permute-start.78 = (bf16[128,1056]{1,0:T(8,128)(2,1)}, bf16[128,1056]{1,0:T(8,128)(2,1)}, u32[]{:S(2)}, u32[]{:S(2)}) collective-permute-start(bf16[128,1056]{1,0:T(8,128)(2,1)} %concatenate.207), channel_id=1, source_target_pairs={{0,8},{8,0},{1,9},{9,1},{2,10},{10,2},{3,11},{11,3},{4,12},{12,4},... | collective-permute-start | bytes 811016 | tf_op jit(solution)/shard_map/ppermute | solution.py:119
  715.9 78.5 %all-to-all-start.6 = ((bf16[16,16,6400]{2,1,0:T(8,128)(2,1)}), bf16[16,16,6400]{2,1,0:T(8,128)(2,1)}, u32[]{:S(2)}, u32[]{:S(2)}) async-start(bf16[16,16,6400]{2,1,0:T(8,128)(2,1)} %get-tuple-element.127), calls=%async_computation.6 | async-start | bytes 6553600 | tf_op jit(solution)/shard_map/all_to_all | solution.py:426
  740.8 47.3 %collective-permute-start.92 = (bf16[160,1536]{1,0:T(8,128)(2,1)}, bf16[160,1536]{1,0:T(8,128)(2,1)S(1)}, u32[]{:S(2)}, u32[]{:S(2)}) collective-permute-start(bf16[160,1536]{1,0:T(8,128)(2,1)} %reduce_sum.171), channel_id=1, source_target_pairs={{0,0},{8,4},{16,8},{24,12},{32,16},{40,20},{48,24},{56,28},{4,32},... | collective-permute-start | bytes 1474568 | tf_op jit(solution)/shard_map/ppermute | solution.py:305
  746.2 55.4 %collective-permute-start.73 = (f32[128,2560]{1,0:T(8,128)}, f32[128,2560]{1,0:T(8,128)S(1)}, u32[]{:S(2)}, u32[]{:S(2)}) collective-permute-start(f32[128,2560]{1,0:T(8,128)} %subtract_add_fusion), channel_id=1, source_target_pairs={{0,0},{4,8},{8,4},{12,12},{1,1},{5,9},{9,5},{13,13},{2,2},{6,10},{... | collective-permute-start | bytes 3932168 | tf_op jit(solution)/shard_map/ppermute | solution.py:123
  753.6 38.6 %collective-permute-start.85 = (bf16[128,1056]{1,0:T(8,128)(2,1)}, bf16[128,1056]{1,0:T(8,128)(2,1)S(1)}, u32[]{:S(2)}, u32[]{:S(2)}) collective-permute-start(bf16[128,1056]{1,0:T(8,128)(2,1)} %collective-permute-done.82), channel_id=1, source_target_pairs={{0,8},{8,0},{1,9},{9,1},{2,10},{10,2},{3,11},{11,3},{4,12},{12,4},... | collective-permute-start | bytes 811016 | tf_op jit(solution)/shard_map/ppermute | solution.py:119
  757.0 33.9 %collective-permute-start.80 = (bf16[128,1056]{1,0:T(8,128)(2,1)}, bf16[128,1056]{1,0:T(8,128)(2,1)S(1)}, u32[]{:S(2)}, u32[]{:S(2)}) collective-permute-start(bf16[128,1056]{1,0:T(8,128)(2,1)} %collective-permute-done.79), channel_id=1, source_target_pairs={{0,8},{8,0},{1,9},{9,1},{2,10},{10,2},{3,11},{11,3},{4,12},{12,4},... | collective-permute-start | bytes 811016 | tf_op jit(solution)/shard_map/ppermute | solution.py:119
  (191 other events, 3206.8 us)

commit v2 on v1

--- a/solution.py
+++ b/solution.py
@@ -145,8 +145,11 @@
 
 
 def gather_group(block):
+    return gather_rest(block, send_z(block, 1), send_z(block, -1))
+
+
+def gather_rest(block, after, before):
     half = block.shape[0] // 2
-    after, before = send_z(block, 1), send_z(block, -1)
     across = jnp.concatenate([send_z(after[:half], 1), send_z(before[half:], -1)], axis=0)
     return [(part, send_core(part)) for part in (block, after, across, before)]
 
@@ -155,30 +158,40 @@
     return jnp.concatenate([part for pair in pairs for part in pair], axis=0)
 
 
-def scatter_ring(sums):
+def ring_across(sums):
     half = sums[0].shape[0] // 2
     across = to_low(sums[2])
-    down = send_z(across[:half], -1).astype(jnp.float32)
-    up = send_z(across[half:], 1).astype(jnp.float32)
-    after = jnp.concatenate([sums[1][:half] + down, sums[1][half:]], axis=0)
-    before = jnp.concatenate([sums[3][:half], sums[3][half:] + up], axis=0)
-    return (
-        sums[0]
-        + send_z(to_low(after), -1).astype(jnp.float32)
-        + send_z(to_low(before), 1).astype(jnp.float32)
-    )
-
-
-def scatter_group(pairs):
-    return scatter_ring(
-        [mine.astype(jnp.float32) + send_core(other).astype(jnp.float32) for mine, other in pairs]
-    )
-
-
-def scatter_halves(mine, other):
+    return send_z(across[:half], -1), send_z(across[half:], 1)
+
+
+def ring_near(sums, down, up):
+    half = sums[0].shape[0] // 2
+    after = jnp.concatenate([sums[1][:half] + down.astype(jnp.float32), sums[1][half:]], axis=0)
+    before = jnp.concatenate([sums[3][:half], sums[3][half:] + up.astype(jnp.float32)], axis=0)
+    return send_z(to_low(after), -1), send_z(to_low(before), 1)
+
+
+def ring_finish(sums, down, up):
+    after, before = ring_near(sums, down, up)
+    return sums[0] + after.astype(jnp.float32) + before.astype(jnp.float32)
+
+
+def halves_sums(mine, other):
     rows = mine.shape[0] // RING
     sums = mine.astype(jnp.float32) + send_core(other).astype(jnp.float32)
-    return scatter_ring([sums[rows * step : rows * (step + 1)] for step in range(RING)])
+    return [sums[rows * step : rows * (step + 1)] for step in range(RING)]
+
+
+def scatter_halves(mine, other):
+    sums = halves_sums(mine, other)
+    return ring_finish(sums, *ring_across(sums))
+
+
+def scatter_group(pairs):
+    sums = [
+        mine.astype(jnp.float32) + send_core(other).astype(jnp.float32) for mine, other in pairs
+    ]
+    return ring_finish(sums, *ring_across(sums))
 
 
 def to_abs(mine, other, place):
@@ -257,19 +270,32 @@
     return second(line, place, send_x, spot_x)
 
 
-def fold(blocks, place, send, spot):
+def fold_across(blocks, place, send, spot):
+    across = lax.dynamic_index_in_dim(blocks, spot(place, 2), axis=0, keepdims=False)
+    half = across.shape[0] // 2
+    return send(across[:half], 1), send(across[half:], -1)
+
+
+def fold_near(blocks, up, down, place, send, spot):
     def at(step):
         return lax.dynamic_index_in_dim(blocks, spot(place, step), axis=0, keepdims=False)
 
-    across, after, before = at(2), at(1), at(3)
-    half = across.shape[0] // 2
-    up = send(across[:half], 1).astype(jnp.float32)
-    down = send(across[half:], -1).astype(jnp.float32)
-    after = after.astype(jnp.float32)
-    before = before.astype(jnp.float32)
-    after = to_low(jnp.concatenate([after[:half] + up, after[half:]], axis=0))
-    before = to_low(jnp.concatenate([before[:half], before[half:] + down], axis=0))
-    parts = (at(0), send(after, 1), send(before, -1))
+    half = up.shape[0]
+    after = at(1).astype(jnp.float32)
+    before = at(3).astype(jnp.float32)
+    after = to_low(jnp.concatenate([after[:half] + up.astype(jnp.float32), after[half:]], axis=0))
+    before = to_low(
+        jnp.concatenate([before[:half], before[half:] + down.astype(jnp.float32)], axis=0)
+    )
+    return at(0), send(after, 1), send(before, -1)
+
+
+def fold(blocks, place, send, spot):
+    up, down = fold_across(blocks, place, send, spot)
+    return fold_sum(fold_near(blocks, up, down, place, send, spot))
+
+
+def fold_sum(parts):
     return to_low(sum(part.astype(jnp.float32) for part in parts))
 
 
@@ -680,9 +706,6 @@
     weights_one = both[:, :cut]
     weights_two = jnp.pad(to_low(down_weight).T, ((0, 0), (0, fill)))
     weights_two = jnp.concatenate([both[:, cut:], weights_two], axis=1)
-    weights_one = trade(weights_one, True)
-    weights_two = trade(weights_two, False)
-    cotangent = swap(out_grad)
     own_pos = (group_index * tok_rows + jnp.arange(tok_rows)).astype(jnp.float32)
     own_cos, own_sin = tables(own_pos)
     factor_one = lax.rsqrt(jnp.mean(tokens * tokens, axis=-1, keepdims=True) + EPS)
@@ -696,7 +719,7 @@
     spaced_other = jnp.where(core_first, spaced[:, :, 1], spaced[:, :, 0]).reshape(tok_rows, -1)
     small = jnp.broadcast_to(small[None], (16,) + small.shape)
     latent_mine, spaced_mine, spaced_other, small = tie(
-        [latent_mine, spaced_mine, spaced_other, small], weights_one, weights_two, cotangent
+        [latent_mine, spaced_mine, spaced_other, small], weights_one, weights_two
     )
     latent_other = send_core(latent_mine)
     small = exchange_plane(small)
@@ -748,14 +771,14 @@
         axis=1,
     )
     packed_pairs = gather_group(packed)
-    cotangent = cotangent.astype(jnp.float32)
     gathered = to_abs([p[0] for p in packed_pairs], [p[1] for p in packed_pairs], place)
+    gathered, small, weights_one, weights_two, out_grad = tie(
+        [gathered, small, weights_one, weights_two, out_grad]
+    )
+    line_one = by_four(four_copies(trade(weights_one, True)), "x")
+    line_two = first_y(trade(weights_two, False), place)
+    cotangent = swap(out_grad).astype(jnp.float32)
     cot_block = to_low(RESIDUAL * cotangent)
-    gathered, cot_block, small, weights_one, weights_two = tie(
-        [gathered, cot_block, small, weights_one, weights_two]
-    )
-    line_one = by_four(four_copies(weights_one), "x")
-    line_two = first_y(weights_two, place)
     cot_all = joined(gather_group(cot_block))
     query_full = unpack_rows(small[:, :, : 3 * wide], wide, wide).reshape(-1, wide)
     keys_matrix = small[:, :, 3 * wide : 3 * wide + key_cols].reshape(-1, key_cols)
@@ -765,13 +788,10 @@
     shared_rot = gathered[:, QR + KVR :]
     factors = rope_slots(seq_rows)
     shared_slot = jnp.pad(shared_rot, ((0, 0), (NOPE, LANES - NOPE - ROPE)))
+    query_lat, line_one, line_two = tie([query_lat, line_one, line_two])
     queries, keys_all, keys_values, attended = attention(
         query_lat, keys_lat, query_full, keys_matrix, factors, shared_slot
     )
-    attended, line_one, line_two, cot_all = tie([attended, line_one, line_two, cot_all])
-    weights_one = by_four(four_copies(line_one), ("yl", "yh")).reshape(D, -1)
-    weights_two = second_x(line_two, place).reshape(D, -1)
-    down_turned = weights_two[:, CELL:]
     attended_mine, attended_other = to_rel(attended, place)
 
     def to_model(rows):
@@ -779,7 +799,12 @@
             jnp.einsum("sa,da->sd", rows, output_turned, preferred_element_type=jnp.float32)
         )
 
-    branch = scatter_halves(to_model(attended_mine), to_model(attended_other))
+    branch_sums = halves_sums(to_model(attended_mine), to_model(attended_other))
+    down, up = ring_across(branch_sums)
+    weights_one = by_four(four_copies(line_one), ("yl", "yh")).reshape(D, -1)
+    weights_two = second_x(line_two, place).reshape(D, -1)
+    down_turned = weights_two[:, CELL:]
+    branch = ring_finish(branch_sums, down, up)
     hidden_state = tokens + RESIDUAL * branch
     mlp_pre, factor_two = rms_forward(hidden_state, gain_two)
 
@@ -807,7 +832,6 @@
         axis=1,
     )
     terms_one = by_four(grad_one.reshape(RING, -1, cut), ("yl", "yh"))
-    grad_mlp_in, grad_two = tie([grad_mlp_in, grad_two], grad_one)
     fold_two = fold_x(grad_two.reshape(RING, -1, grad_two.shape[1]), place)
 
     grad_norm_two, grad_gain_two = rms_backward(grad_mlp_in, hidden_state, factor_two, gain_two)
@@ -888,21 +912,17 @@
             axis=1,
         )
     )
-    latent_terms, block_output, small_grads, terms_one, fold_two = tie(
-        [latent_terms, block_output, small_grads, terms_one, fold_two]
-    )
-    block_output = swap(block_output)
+    latent_terms, block_output, small_grads, terms_one = tie(
+        [latent_terms, block_output, small_grads, terms_one]
+    )
     terms_one = by_four(add_up(terms_one).reshape(RING, -1, cut), "x")
+    grad_latent_in = scatter_halves(*to_rel(latent_terms, place))
+    grad_latent_in, small_grads, terms_one, fold_two = tie(
+        [grad_latent_in, small_grads, terms_one, fold_two]
+    )
+    small_terms = exchange_plane(small_grads)
+    sum_one = trade_back(add_up(terms_one), True)
     sum_two = trade_back(fold_y(fold_two.reshape(RING, -1, fold_two.shape[1]), place), False)
-    sum_down = sum_two[:, CELL : CELL + hidden_here].astype(jnp.float32).T
-    grad_latent_in = scatter_halves(*to_rel(latent_terms, place))
-    grad_latent_in, small_grads, terms_one = tie([grad_latent_in, small_grads, terms_one])
-    sum_one = trade_back(add_up(terms_one), True)
-    sum_gate, sum_up = (
-        part[:, :hidden_here].astype(jnp.float32)
-        for part in unmix(jnp.concatenate([sum_one, sum_two[:, :CELL]], axis=1))
-    )
-    small_terms = exchange_plane(small_grads)
     grad_query_pre, grad_gain_query = rms_backward(
         grad_latent_in[:, :QR], query_part, factor_query, gain_query
     )
@@ -915,9 +935,11 @@
         "sc,dc->sd", grad_latent, latent_full, preferred_element_type=jnp.float32
     )
     grad_norm_one, grad_gain_one = rms_backward(grad_normed, tokens, factor_one, gain_one)
-    input_grad = swap(grad_state + grad_norm_one)
+    input_grad = swap(to_low(grad_state + grad_norm_one)).astype(jnp.float32)
 
     latent_grads = joined(gather_group(grad_latent))
+    latent_grads, block_output = tie([latent_grads, block_output])
+    block_output = swap(to_low(block_output)).astype(jnp.float32)
     grad_latent_w = jnp.einsum(
         "sd,sc->dc",
         normed_all,
@@ -942,7 +964,12 @@
         gains_sum = gains_sum + send_z(gains_at(step), step)
     gains_rows = jnp.pad(gains_sum.reshape(16, 1, gain_width), ((0, 0), (0, 0), (0, width - gain_width)))
     last = to_low(jnp.concatenate([grad_latent_w.reshape(16, -1, width), gains_rows], axis=1))
-    last, small_terms = tie([last, small_terms])
+    last, small_terms, sum_one, sum_two = tie([last, small_terms, sum_one, sum_two])
+    sum_down = sum_two[:, CELL : CELL + hidden_here].astype(jnp.float32).T
+    sum_gate, sum_up = (
+        part[:, :hidden_here].astype(jnp.float32)
+        for part in unmix(jnp.concatenate([sum_one, sum_two[:, :CELL]], axis=1))
+    )
     sum_small = swap(add_up(small_terms)).astype(jnp.float32)
     sum_query = from_slots(unpack_rows(sum_small[None, :, : 3 * wide], wide, wide)[0])
     sum_keys = sum_small[:, 3 * wide : 3 * wide + key_cols]

time: 856 us -> 851 us (level)
  waiting for transfers between devices: 233 us -> 191 us
  other arithmetic: 117 us -> 135 us
  starting transfers between devices: 193 us -> 208 us
  local copies, waits for them, and re-layouts: 152 us -> 164 us
  matrix products: 82.6 us -> 72.9 us
    ppermute x2, waiting for transfers between devices: 38.7 us -> 0.01 us  [trade_back(): return lax.ppermute(block, ('yl', 'x', 'c', 'yh'), back)]
    ppermute x6, waiting for transfers between devices: 43 us -> 5.69 us  [swap(): return lax.ppermute(block, ('c', 'yh'), [(0, 0), (1, 2), (2, 1), (3, 3)])]
    all_to_all x1, waiting for transfers between devices: 0.01 us -> 27.1 us  [shards(): lax.all_to_all(jnp.broadcast_to(latent_block[None], (64,) + latent_block....]
    ppermute x7, waiting for transfers between devices: 4.67 us -> 26.2 us  [send_y(): return lax.ppermute(block, ('yl', 'yh'), pairs)]
    ppermute x8, waiting for transfers between devices: 28.8 us -> 9.83 us  [send_x(): return lax.ppermute(block, 'x', ring(step))]
    all_to_all x3, waiting for transfers between devices: 42 us -> 29.4 us  [exchange_plane(): lax.all_to_all(blocks, PLANE, split_axis=0, concat_axis=0, tiled=True)]
    ppermute x30, starting transfers between devices: 32.6 us -> 43.4 us  [send_core(): return lax.ppermute(block, 'c', [(0, 1), (1, 0)])]
    ppermute x42, waiting for transfers between devices: 55 us -> 65 us  [send_z(): return lax.ppermute(block, 'z', ring(step))]
  transfers between devices with their start and end apart: 106 -> 106, of which waited for: 32 -> 32; matrix products, arithmetic and copies ran while one was open for 33% -> 37% of each run, Pallas kernels for 5% -> 5%
where the time goes in v2:
time: 851 us; the launch traced here: 836 us
  starting transfers between devices  208 us (24%)
  waiting for transfers between devices  191 us (22%)
  local copies, waits for them, and re-layouts  164 us (19%)
  other arithmetic  135 us (16%)
  matrix products  72.9 us (9%)
  Pallas kernels  60.8 us (7%)
    ppermute x42, waiting for transfers between devices, send_z(): return lax.ppermute(block, 'z', ring(step))  65 us
    ppermute x42, starting transfers between devices, send_z(): return lax.ppermute(block, 'z', ring(step))  52.9 us
    unnamed x242, local copies, waits for them, and re-layouts  48.6 us
    ppermute x30, starting transfers between devices, send_core(): return lax.ppermute(block, 'c', [(0, 1), (1, 0)])  43.4 us
    pallas_call x2, Pallas kernels, feed_forward(): pl.pallas_call(ff_kernel, grid=(steps,), in_specs=[whole] * 4 + [pl.Block...  34.1 us
    all_to_all x3, waiting for transfers between devices, exchange_plane(): lax.all_to_all(blocks, PLANE, split_axis=0, concat_axis=0, tiled=True)  29.4 us
    all_to_all x1, waiting for transfers between devices, shards(): lax.all_to_all(jnp.broadcast_to(latent_block[None], (64,) + latent_block....  27.1 us
    ppermute x7, waiting for transfers between devices, send_y(): return lax.ppermute(block, ('yl', 'yh'), pairs)  26.2 us
  transfers between devices with their start and end apart: 106, of which 32 were waited for; matrix products, arithmetic and copies ran while one was open for 37% of the time, Pallas kernels for 5%

profile of v2, /device:TPU:5, one launch (start us, length us, event | category | flops | bytes accessed | tf_op | source)
XLA Modules:
  0.0 835.7 jit_solution(403951915343725248)
XLA Ops:
  6.4 5.4 collective-permute-start.1
  15.8 13.5 %all-to-all-start = ((bf16[64,24,1056]{2,1,0:T(8,128)(2,1)}), bf16[64,24,1056]{2,1,0:T(8,128)(2,1)S(1)}, u32[]{:S(2)}, u32[]{:S(2)}) async-start(bf16[64,24,1056]{2,1,0:T(8,128)(2,1)} %broadcast_in_dim.25), calls=%async_computation | async-start | bytes 7077888 | tf_op jit(solution)/shard_map/all_to_all | solution.py:680
  52.7 27.1 %all-to-all-done.refs_0_ = bf16[64,24,1056]{2,1,0:T(8,128)(2,1)S(1)} async-done(((bf16[64,24,1056]{2,1,0:T(8,128)(2,1)}), bf16[64,24,1056]{2,1,0:T(8,128)(2,1)S(1)}, u32[]{:S(2)}, u32[]{:S(2)}) %all-to-all-start) | async-done | bytes 3244064 | tf_op jit(solution)/shard_map/all_to_all | solution.py:680
  98.6 7.8 all-to-all-start.1
  127.5 29.4 %all-to-all-done.1.refs_1_ = bf16[16,16,6400]{2,1,0:T(8,128)(2,1)} async-done(((bf16[16,16,6400]{2,1,0:T(8,128)(2,1)}), bf16[16,16,6400]{2,1,0:T(8,128)(2,1)}, u32[]{:S(2)}, u32[]{:S(2)}) %all-to-all-start.1) | async-done | bytes 3276832 | tf_op jit(solution)/shard_map/all_to_all | solution.py:452
  163.3 7.2 pad_maximum_fusion
  170.5 10.2 %reshape.380.refs_1_ = bf16[2560,1056]{1,0:T(8,128)(2,1)} reshape(bf16[8,2,8,20,1056]{4,3,2,1,0:T(8,128)(2,1)} %pad_maximum_fusion) | data formatting | bytes 10813440 | tf_op jit(solution)/shard_map/reshape | solution.py:744
  190.2 5.7 collective-permute-start.12
  251.6 10.6 %attention.1 = (bf16[1024,640]{1,0:T(8,128)(2,1)S(1)}, bf16[1024,640]{1,0:T(8,128)(2,1)}, bf16[1024,640]{1,0:T(8,128)(2,1)}, bf16[1024,320]{1,0:T(8,128)(2,1)S(1)}) custom-call(bf16[1024,768]{1,0:T(8,128)(2,1)} %get-tuple-element.87.query_ref, bf16[1024,256]{1,0:T(8,128)(2,1)S(1)} %slice.498.keys_ref, bf16[768,640]{1,0:T(8,128)(2,1)S(1)} %bitcast.233, ...), custom_call_target="tpu_custom_call" | custom-call | flops 2684354560 | bytes 8388608 | tf_op jit(solution)/shard_map/attention/pallas_call | solution.py:524
  276.7 5.5 broadcast_in_dim.35
  282.2 5.5 all-to-all-start.3
  322.8 5.6 collective-permute-done.21
  346.7 8.7 %fusion.2.refs_0_ = f32[1024,896]{1,0:T(8,128)} fusion(bf16[1024,2560]{1,0:T(8,128)(2,1)} %constant_dynamic-update-slice_fusion.2, bf16[2560,1152]{1,0:T(8,128)(2,1)S(1)} %bitcast.255), kind=kOutput, calls=%fused_computation.16 | convolution fusion | flops 4697620480 | bytes 13500416 | tf_op jit(solution)/shard_map/dot_general | solution.py:812
  377.9 16.6 %feed_forward.2 = (bf16[128,2560]{1,0:T(8,128)(2,1)S(1)}, bf16[128,2560]{1,0:T(8,128)(2,1)}, bf16[128,2560]{1,0:T(8,128)(2,1)S(1)}, bf16[128,2560]{1,0:T(8,128)(...) custom-call(bf16[128,2560]{1,0:T(8,128)(2,1)S(1)} %multiply_convert_fusion.2.refs_0_, ...), custom_call_target="tpu_custom_call" | custom-call | flops 9395240960 | bytes 20971520 | tf_op jit(solution)/shard_map/feed_forward/pallas_call | solution.py:395
  394.5 17.5 %feed_forward.3 = (bf16[128,2560]{1,0:T(8,128)(2,1)S(1)}, bf16[128,2560]{1,0:T(8,128)(2,1)}, bf16[128,2560]{1,0:T(8,128)(2,1)S(1)}, bf16[128,2560]{1,0:T(8,128)(...) custom-call(bf16[128,2560]{1,0:T(8,128)(2,1)} %constant_dynamic-upda, ...), custom_call_target="tpu_custom_call", output_to_operand_aliasing={{4}: (7, {}), {5}: (8, {}), {6}: (9, {})} | custom-call | flops 9395240960 | bytes 20971520 | tf_op jit(solution)/shard_map/feed_forward/pallas_call | solution.py:395
  417.3 10.3 %convolution_convert_fusion = bf16[2560,1536]{1,0:T(8,128)(2,1)} fusion(bf16[1024,2560]{1,0:T(8,128)(2,1)S(1)} %copy-done.98, bf16[1024,1792]{1,0:T(8,128)(2,1)S(1)} %copy-done.99), kind=kOutput, calls=%fused_computation | convolution fusion | flops 8056995840 | bytes 16252928 | tf_op jit(solution)/shard_map/sd,sf->df/dot_general | solution.py:825
  427.7 7.5 convolution_convert_fusion.1
  439.6 8.8 %copy.209 = bf16[2560,1152]{1,0:T(8,128)(2,1)} copy(bf16[2560,1152]{0,1:T(8,128)(2,1)} %pad_maximum_fusion.1) | data formatting | bytes 11796480 | tf_op jit(solution)/shard_map/concatenate | solution.py:827
  448.4 5.6 all-to-all-start.4
  479.7 6.6 collective-permute-done.46
  545.5 16.1 %attention_back.1 = (bf16[1024,640]{1,0:T(8,128)(2,1)S(1)}, bf16[1024,640]{1,0:T(8,128)(2,1)S(1)}, f32[1024,128]{1,0:T(8,128)S(1)}) custom-call(bf16[1024,640]{1,0:T(8,128)(2,1)} %copy-done.14, bf16[1024,640]{1,0:T(8,128)(2,1)} %get-tuple-element.90.k_ref, bf16[1024,640]{1,0:T(8,128)(2,1)} %get-tuple-element.91.kv_ref, bf16[1024,320]{1,0:T(8,128)(2,1)S(1)} %copy-done, ...), custom_call_target="tpu_custom_call" | custom-call | flops 6710886400 | bytes 10485760 | tf_op jit(solution)/shard_map/attention_back/pallas_call | solution.py:600
  582.4 5.7 collective-permute-done.59
  594.1 11.4 %collective-permute-done.62 = bf16[128,2560]{1,0:T(8,128)(2,1)S(1)} collective-permute-done((bf16[128,2560]{1,0:T(8,128)(2,1)S(1)}, bf16[128,2560]{1,0:T(8,128)(2,1)S(1)}, u32[]{:S(2)}, u32[]{:S(2)}) %collective-permute-start.62) | collective-permute-done | bytes 655392 | tf_op jit(solution)/shard_map/ppermute | solution.py:106
  636.6 6.3 reduce_sum.161
  642.9 5.6 all-to-all-start.5
  664.9 12.7 %all-to-all-done.5.refs_2_ = bf16[4,160,1536]{2,1,0:T(8,128)(2,1)S(1)} async-done(((bf16[4,160,1536]{2,1,0:T(8,128)(2,1)}), bf16[4,160,1536]{2,1,0:T(8,128)(2,1)S(1)}, u32[]{:S(2)}, u32[]{:S(2)}) %all-to-all-start.5) | async-done | bytes 1966112 | tf_op jit(solution)/shard_map/all_to_all | solution.py:335
  685.6 6.2 all-to-all-start.6
  695.8 6.0 fusion.16
  721.8 21.9 %collective-permute-done.91 = bf16[80,1152]{1,0:T(8,128)(2,1)} collective-permute-done((bf16[80,1152]{1,0:T(8,128)(2,1)}, bf16[80,1152]{1,0:T(8,128)(2,1)}, u32[]{:S(2)}, u32[]{:S(2)}) %collective-permute-start.91) | collective-permute-done | bytes 184352 | tf_op jit(solution)/shard_map/ppermute | solution.py:115
  790.4 5.7 collective-permute-done.80
  806.6 6.9 collective-permute-start.97
  827.9 6.2 collective-permute-done.96
  (694 shorter events, 506.6 us)
Async XLA Ops:
  6.4 46.3 %collective-permute-start.1 = (bf16[16,6400]{1,0:T(8,128)(2,1)}, bf16[16,6400]{1,0:T(8,128)(2,1)}, u32[]{:S(2)}, u32[]{:S(2)}) collective-permute-start(bf16[16,6400]{1,0:T(8,128)(2,1)} %pad_maximum_fusion.38), channel_id=1, source_target_pairs={{0,0},{4,8},{8,4},{12,12},{1,1},{5,9},{9,5},{13,13},{2,2},{6,10},{... | collective-permute-start | bytes 614408 | tf_op jit(solution)/shard_map/ppermute | solution.py:123
  15.8 64.0 %all-to-all-start = ((bf16[64,24,1056]{2,1,0:T(8,128)(2,1)}), bf16[64,24,1056]{2,1,0:T(8,128)(2,1)S(1)}, u32[]{:S(2)}, u32[]{:S(2)}) async-start(bf16[64,24,1056]{2,1,0:T(8,128)(2,1)} %broadcast_in_dim.25), calls=%async_computation | async-start | bytes 7077888 | tf_op jit(solution)/shard_map/all_to_all | solution.py:680
  98.6 58.3 %all-to-all-start.1 = ((bf16[16,16,6400]{2,1,0:T(8,128)(2,1)}), bf16[16,16,6400]{2,1,0:T(8,128)(2,1)}, u32[]{:S(2)}, u32[]{:S(2)}) async-start(bf16[16,16,6400]{2,1,0:T(8,128)(2,1)} %get-tuple-element.83), calls=%async_computation.1 | async-start | bytes 6553600 | tf_op jit(solution)/shard_map/all_to_all | solution.py:452
  156.9 58.8 %collective-permute-start.11 = (bf16[160,1536]{1,0:T(8,128)(2,1)}, bf16[160,1536]{1,0:T(8,128)(2,1)}, u32[]{:S(2)}, u32[]{:S(2)}) collective-permute-start(bf16[160,1536]{1,0:T(8,128)(2,1)} %get-tuple-element.85), channel_id=1, source_target_pairs={{0,0},{4,8},{8,16},{12,24},{16,32},{20,40},{24,48},{28,56},{32,4},... | collective-permute-start | bytes 1474568 | tf_op jit(solution)/shard_map/ppermute | solution.py:326
  161.3 61.3 %collective-permute-start.16 = (bf16[128,2560]{1,0:T(8,128)(2,1)}, bf16[128,2560]{1,0:T(8,128)(2,1)}, u32[]{:S(2)}, u32[]{:S(2)}) collective-permute-start(bf16[128,2560]{1,0:T(8,128)(2,1)} %get-tuple-element.92), channel_id=1, source_target_pairs={{0,0},{4,8},{8,4},{12,12},{1,1},{5,9},{9,5},{13,13},{2,2},{6,10},{... | collective-permute-start | bytes 1966088 | tf_op jit(solution)/shard_map/ppermute | solution.py:123
  218.2 32.5 %all-to-all-start.2 = ((bf16[4,160,1536]{2,1,0:T(8,128)(2,1)}), bf16[4,160,1536]{2,1,0:T(8,128)(2,1)}, u32[]{:S(2)}, u32[]{:S(2)}) async-start(bf16[4,160,1536]{2,1,0:T(8,128)(2,1)} %broadcast_in_dim.27), calls=%async_computation.2 | async-start | bytes 3932160 | tf_op jit(solution)/shard_map/all_to_all | solution.py:335
  239.4 26.5 %collective-permute-start.30 = (bf16[64,2560]{1,0:T(8,128)(2,1)}, bf16[64,2560]{1,0:T(8,128)(2,1)}, u32[]{:S(2)}, u32[]{:S(2)}) collective-permute-start(bf16[64,2560]{1,0:T(8,128)(2,1)} %slice.640), channel_id=1, source_target_pairs={{0,3},{1,0},{2,1},{3,2},{4,7},{5,4},{6,5},{7,6},{8,11},{9,8},{10,9... | collective-permute-start | bytes 983048 | tf_op jit(solution)/shard_map/ppermute | solution.py:106
  243.1 72.5 %collective-permute-start.32 = (bf16[128,2560]{1,0:T(8,128)(2,1)}, bf16[128,2560]{1,0:T(8,128)(2,1)}, u32[]{:S(2)}, u32[]{:S(2)}) collective-permute-start(bf16[128,2560]{1,0:T(8,128)(2,1)} %collective-permute-done.29), channel_id=1, source_target_pairs={{0,8},{8,0},{1,9},{9,1},{2,10},{10,2},{3,11},{11,3},{4,12},{12,4},... | collective-permute-start | bytes 1966088 | tf_op jit(solution)/shard_map/ppermute | solution.py:119
  247.4 41.6 %collective-permute-start.27 = (bf16[128,2560]{1,0:T(8,128)(2,1)}, bf16[128,2560]{1,0:T(8,128)(2,1)}, u32[]{:S(2)}, u32[]{:S(2)}) collective-permute-start(bf16[128,2560]{1,0:T(8,128)(2,1)} %collective-permute-done.26), channel_id=1, source_target_pairs={{0,8},{8,0},{1,9},{9,1},{2,10},{10,2},{3,11},{11,3},{4,12},{12,4},... | collective-permute-start | bytes 1966088 | tf_op jit(solution)/shard_map/ppermute | solution.py:119
  265.4 31.3 %collective-permute-start.17 = (bf16[512,2560]{1,0:T(8,128)(2,1)}, bf16[512,2560]{1,0:T(8,128)(2,1)}, u32[]{:S(2)}, u32[]{:S(2)}) collective-permute-start(bf16[512,2560]{1,0:T(8,128)(2,1)} %convolution_convert_fusion.4), channel_id=1, source_target_pairs={{0,8},{8,0},{1,9},{9,1},{2,10},{10,2},{3,11},{11,3},{4,12},{12,4},... | collective-permute-start | bytes 7864328 | tf_op jit(solution)/shard_map/ppermute | solution.py:119
  267.9 26.9 %collective-permute-start.31 = (bf16[128,2560]{1,0:T(8,128)(2,1)}, bf16[128,2560]{1,0:T(8,128)(2,1)}, u32[]{:S(2)}, u32[]{:S(2)}) collective-permute-start(bf16[128,2560]{1,0:T(8,128)(2,1)} %pad_maximum_fusion.14), channel_id=1, source_target_pairs={{0,8},{8,0},{1,9},{9,1},{2,10},{10,2},{3,11},{11,3},{4,12},{12,4},... | collective-permute-start | bytes 1966088 | tf_op jit(solution)/shard_map/ppermute | solution.py:119
  267.9 49.7 %collective-permute-start.35 = (bf16[4,160,1152]{2,1,0:T(8,128)(2,1)S(1)}, bf16[4,160,1152]{2,1,0:T(8,128)(2,1)}, u32[]{:S(2)}, u32[]{:S(2)}) collective-permute-start(bf16[4,160,1152]{2,1,0:T(8,128)(2,1)S(1)} %copy-done.25), channel_id=1, source_target_pairs={{0,48},{16,0},{32,16},{48,32},{1,49},{17,1},{33,17},{49,33},{2,50}... | collective-permute-start | bytes 4423688 | tf_op jit(solution)/shard_map/ppermute | solution.py:110
  282.2 93.6 %all-to-all-start.3 = ((bf16[4,4,160,1536]{3,2,1,0:T(8,128)(2,1)}), bf16[4,4,160,1536]{3,2,1,0:T(8,128)(2,1)}, u32[]{:S(2)}, u32[]{:S(2)}) async-start(bf16[4,4,160,1536]{3,2,1,0:T(8,128)(2,1)} %broadcast_in_dim.35), calls=%async_computation.3 | async-start | bytes 15728640 | tf_op jit(solution)/shard_map/all_to_all | solution.py:335
  289.0 33.2 %collective-permute-start.33 = (bf16[4,160,1152]{2,1,0:T(8,128)(2,1)S(1)}, bf16[4,160,1152]{2,1,0:T(8,128)(2,1)S(1)}, u32[]{:S(2)}, u32[]{:S(2)}) collective-permute-start(bf16[4,160,1152]{2,1,0:T(8,128)(2,1)S(1)} %copy-done.25), channel_id=1, source_target_pairs={{0,16},{16,32},{32,48},{48,0},{1,17},{17,33},{33,49},{49,1},{2,18}... | collective-permute-start | bytes 4423688 | tf_op jit(solution)/shard_map/ppermute | solution.py:110
  363.1 31.3 %collective-permute-start.43 = (bf16[128,2560]{1,0:T(8,128)(2,1)}, bf16[128,2560]{1,0:T(8,128)(2,1)}, u32[]{:S(2)}, u32[]{:S(2)}) collective-permute-start(bf16[128,2560]{1,0:T(8,128)(2,1)} %collective-permute-done.40.refs_2_), channel_id=1, source_target_pairs={{0,8},{8,0},{1,9},{9,1},{2,10},{10,2},{3,11},{11,3},{4,12},{12,4},... | collective-permute-start | bytes 1966088 | tf_op jit(solution)/shard_map/ppermute | solution.py:119
  435.1 44.6 %collective-permute-start.37 = (bf16[128,2560]{1,0:T(8,128)(2,1)}, bf16[128,2560]{1,0:T(8,128)(2,1)}, u32[]{:S(2)}, u32[]{:S(2)}) collective-permute-start(bf16[128,2560]{1,0:T(8,128)(2,1)} %get-tuple-element.98), channel_id=1, source_target_pairs={{0,8},{8,0},{1,9},{9,1},{2,10},{10,2},{3,11},{11,3},{4,12},{12,4},... | collective-permute-start | bytes 1966088 | tf_op jit(solution)/shard_map/ppermute | solution.py:119
  436.6 26.9 %collective-permute-start.47 = (bf16[128,2560]{1,0:T(8,128)(2,1)}, bf16[128,2560]{1,0:T(8,128)(2,1)}, u32[]{:S(2)}, u32[]{:S(2)}) collective-permute-start(bf16[128,2560]{1,0:T(8,128)(2,1)} %get-tuple-element.107), channel_id=1, source_target_pairs={{0,8},{8,0},{1,9},{9,1},{2,10},{10,2},{3,11},{11,3},{4,12},{12,4},... | collective-permute-start | bytes 1966088 | tf_op jit(solution)/shard_map/ppermute | solution.py:119
  448.4 158.6 %all-to-all-start.4 = ((bf16[4,640,1536]{2,1,0:T(8,128)(2,1)}), bf16[4,640,1536]{2,1,0:T(8,128)(2,1)}, u32[]{:S(2)}, u32[]{:S(2)}) async-start(bf16[4,640,1536]{2,1,0:T(8,128)(2,1)} %bitcast.251), calls=%async_computation.4 | async-start | bytes 15728640 | tf_op jit(solution)/shard_map/all_to_all | solution.py:335
  473.8 30.2 %collective-permute-start.68 = (bf16[320,1152]{1,0:T(8,128)(2,1)S(1)}, bf16[320,1152]{1,0:T(8,128)(2,1)S(1)}, u32[]{:S(2)}, u32[]{:S(2)}) collective-permute-start(bf16[320,1152]{1,0:T(8,128)(2,1)S(1)} %get-tuple-element.177), channel_id=1, source_target_pairs={{0,16},{16,32},{32,48},{48,0},{1,17},{17,33},{33,49},{49,1},{2,18}... | collective-permute-start | bytes 2211848 | tf_op jit(solution)/shard_map/ppermute | solution.py:110
  474.1 29.9 %collective-permute-start.70 = (bf16[320,1152]{1,0:T(8,128)(2,1)S(1)}, bf16[320,1152]{1,0:T(8,128)(2,1)S(1)}, u32[]{:S(2)}, u32[]{:S(2)}) collective-permute-start(bf16[320,1152]{1,0:T(8,128)(2,1)S(1)} %get-tuple-element.179), channel_id=1, source_target_pairs={{0,48},{16,0},{32,16},{48,32},{1,49},{17,1},{33,17},{49,33},{2,50}... | collective-permute-start | bytes 2211848 | tf_op jit(solution)/shard_map/ppermute | solution.py:110
  538.9 37.3 %collective-permute-start.58 = (bf16[512,2560]{1,0:T(8,128)(2,1)}, bf16[512,2560]{1,0:T(8,128)(2,1)}, u32[]{:S(2)}, u32[]{:S(2)}) collective-permute-start(bf16[512,2560]{1,0:T(8,128)(2,1)} %get-tuple-element.115), channel_id=1, source_target_pairs={{0,8},{8,0},{1,9},{9,1},{2,10},{10,2},{3,11},{11,3},{4,12},{12,4},... | collective-permute-start | bytes 7864328 | tf_op jit(solution)/shard_map/ppermute | solution.py:119
  614.7 41.3 %collective-permute-start.71 = (bf16[640,1152]{1,0:T(8,128)(2,1)}, bf16[640,1152]{1,0:T(8,128)(2,1)}, u32[]{:S(2)}, u32[]{:S(2)}) collective-permute-start(bf16[640,1152]{1,0:T(8,128)(2,1)} %pad_maximum_fusion.7), channel_id=1, source_target_pairs={{0,48},{16,0},{32,16},{48,32},{1,49},{17,1},{33,17},{49,33},{2,50}... | collective-permute-start | bytes 4423688 | tf_op jit(solution)/shard_map/ppermute | solution.py:110
  622.2 33.8 %collective-permute-start.69 = (bf16[640,1152]{1,0:T(8,128)(2,1)}, bf16[640,1152]{1,0:T(8,128)(2,1)S(1)}, u32[]{:S(2)}, u32[]{:S(2)}) collective-permute-start(bf16[640,1152]{1,0:T(8,128)(2,1)} %pad_maximum_fusion.6), channel_id=1, source_target_pairs={{0,16},{16,32},{32,48},{48,0},{1,17},{17,33},{33,49},{49,1},{2,18}... | collective-permute-start | bytes 4423688 | tf_op jit(solution)/shard_map/ppermute | solution.py:110
  642.9 34.6 %all-to-all-start.5 = ((bf16[4,160,1536]{2,1,0:T(8,128)(2,1)}), bf16[4,160,1536]{2,1,0:T(8,128)(2,1)S(1)}, u32[]{:S(2)}, u32[]{:S(2)}) async-start(bf16[4,160,1536]{2,1,0:T(8,128)(2,1)} %bitcast.249), calls=%async_computation.5 | async-start | bytes 3932160 | tf_op jit(solution)/shard_map/all_to_all | solution.py:335
  685.6 111.6 %all-to-all-start.6 = ((bf16[16,16,6400]{2,1,0:T(8,128)(2,1)}), bf16[16,16,6400]{2,1,0:T(8,128)(2,1)S(1)}, u32[]{:S(2)}, u32[]{:S(2)}) async-start(bf16[16,16,6400]{2,1,0:T(8,128)(2,1)} %get-tuple-element.127), calls=%async_computation.6 | async-start | bytes 6553600 | tf_op jit(solution)/shard_map/all_to_all | solution.py:452
  706.4 37.3 %collective-permute-start.91 = (bf16[80,1152]{1,0:T(8,128)(2,1)}, bf16[80,1152]{1,0:T(8,128)(2,1)}, u32[]{:S(2)}, u32[]{:S(2)}) collective-permute-start(bf16[80,1152]{1,0:T(8,128)(2,1)} %get-tuple-element.215), channel_id=1, source_target_pairs={{0,64},{64,4},{4,68},{68,0},{1,65},{65,5},{5,69},{69,1},{2,66},{66... | collective-permute-start | bytes 552968 | tf_op jit(solution)/shard_map/ppermute | solution.py:115
  707.6 40.2 %collective-permute-start.93 = (bf16[80,1152]{1,0:T(8,128)(2,1)}, bf16[80,1152]{1,0:T(8,128)(2,1)}, u32[]{:S(2)}, u32[]{:S(2)}) collective-permute-start(bf16[80,1152]{1,0:T(8,128)(2,1)} %get-tuple-element.217), channel_id=1, source_target_pairs={{0,68},{64,0},{4,64},{68,4},{1,69},{65,1},{5,65},{69,5},{2,70},{66... | collective-permute-start | bytes 552968 | tf_op jit(solution)/shard_map/ppermute | solution.py:115
  718.5 36.1 %collective-permute-start.76 = (bf16[128,1056]{1,0:T(8,128)(2,1)}, bf16[128,1056]{1,0:T(8,128)(2,1)}, u32[]{:S(2)}, u32[]{:S(2)}) collective-permute-start(bf16[128,1056]{1,0:T(8,128)(2,1)} %concatenate.207), channel_id=1, source_target_pairs={{0,3},{1,0},{2,1},{3,2},{4,7},{5,4},{6,5},{7,6},{8,11},{9,8},{10,9... | collective-permute-start | bytes 811016 | tf_op jit(solution)/shard_map/ppermute | solution.py:106
  719.8 37.0 %collective-permute-start.73 = (bf16[128,1056]{1,0:T(8,128)(2,1)}, bf16[128,1056]{1,0:T(8,128)(2,1)}, u32[]{:S(2)}, u32[]{:S(2)}) collective-permute-start(bf16[128,1056]{1,0:T(8,128)(2,1)} %concatenate.207), channel_id=1, source_target_pairs={{0,1},{1,2},{2,3},{3,0},{4,5},{5,6},{6,7},{7,4},{8,9},{9,10},{10,1... | collective-permute-start | bytes 811016 | tf_op jit(solution)/shard_map/ppermute | solution.py:106
  719.9 38.1 %collective-permute-start.72 = (bf16[128,1056]{1,0:T(8,128)(2,1)}, bf16[128,1056]{1,0:T(8,128)(2,1)}, u32[]{:S(2)}, u32[]{:S(2)}) collective-permute-start(bf16[128,1056]{1,0:T(8,128)(2,1)} %concatenate.207), channel_id=1, source_target_pairs={{0,8},{8,0},{1,9},{9,1},{2,10},{10,2},{3,11},{11,3},{4,12},{12,4},... | collective-permute-start | bytes 811016 | tf_op jit(solution)/shard_map/ppermute | solution.py:119
  743.7 53.5 %collective-permute-start.90 = (bf16[160,1536]{1,0:T(8,128)(2,1)}, bf16[160,1536]{1,0:T(8,128)(2,1)}, u32[]{:S(2)}, u32[]{:S(2)}) collective-permute-start(bf16[160,1536]{1,0:T(8,128)(2,1)} %reduce_sum.169), channel_id=1, source_target_pairs={{0,0},{8,4},{16,8},{24,12},{32,16},{40,20},{48,24},{56,28},{4,32},... | collective-permute-start | bytes 1474568 | tf_op jit(solution)/shard_map/ppermute | solution.py:331
  747.8 36.4 %collective-permute-start.81 = (bf16[128,2560]{1,0:T(8,128)(2,1)}, bf16[128,2560]{1,0:T(8,128)(2,1)}, u32[]{:S(2)}, u32[]{:S(2)}) collective-permute-start(bf16[128,2560]{1,0:T(8,128)(2,1)} %add_convert_fusion), channel_id=1, source_target_pairs={{0,0},{4,8},{8,4},{12,12},{1,1},{5,9},{9,5},{13,13},{2,2},{6,10},{... | collective-permute-start | bytes 1966088 | tf_op jit(solution)/shard_map/ppermute | solution.py:123
  (178 other events, 2430.2 us)
